TPU v7x, 256 devices: a whole 4x4x8 slice. The times are simulated.
256 devices in a mesh: row: 16 (over z, core), col: 16 (over y, x).
Axes of the slice: x: 4, y: 4, z: 8, core: 2. Of those that a mesh axis runs over, the one named last changes fastest.
Arguments:
- vectors: bfloat16 [16, 131072], P(None, ('row', 'col')), may hold values from -0.5 to 1.5
- degrees: int32 [131072], P(('row', 'col')), may hold values from 1 to 10, as said below
- hub_ids: int32 [1024], replicated, may hold values from 0 to 131071, as said below
- hub_weight: bfloat16 [1024, 131072], P(None, ('row', 'col')), may hold values from -0.1796875 to 0.1796875
- tile_values: bfloat16 [24576, 128, 128], P(('row', 'col')), may hold values from -0.8984375 to 0.8984375
- tile_rows: int32 [24576], P(('row', 'col')), may hold values from 0 to 63, as said below
- tile_cols: int32 [24576, 128], P(('row', 'col')), may hold values from 0 to 8191
Outputs:
- basis: float32 [16, 131072], P(None, ('row', 'col'))
- factor: float32 [16, 16], replicated
Inputs may be any that keep to these rules, and one draw needn't show every extreme that they name: degrees tend to rise with the vertex id. `hub_ids`: distinct vertex ids; the vertices of each device hold exactly 1024 / (16 * 16) hubs, and the list names them device by device: hub h lies on device h // (1024 / (16 * 16)). `tile_rows`: among the 96 tiles of one device every tile row of its row block is named at least once.
All inputs are finite; a program needn't handle non-finite values.
Results may differ from a plain program's by a relative error of at most 0.0003.
Values may be sent and summed in bfloat16 or wider, within the bound.
No kernel may reach another device: no remote copies, remote signals or barrier semaphores. Data moves between devices by JAX's collectives and lax.ppermute only.
A program may use at most 64 MiB of HBM per device.

v0:
```python
import jax
import jax.numpy as jnp
from jax import lax
from jax.sharding import PartitionSpec as P


def on_device(vectors, degrees, hub_ids, hub_weight, tile_values, tile_rows, tile_cols):
    count = vectors.shape[0]
    width = vectors.shape[1]
    tile = tile_values.shape[1]
    tile_count = tile_values.shape[0]
    cols_n = lax.axis_size("col")
    rows_n = lax.axis_size("row")
    piece = lax.axis_index("row") * cols_n + lax.axis_index("col")
    offset = hub_ids - piece * width
    inside = ((offset >= 0) & (offset < width)).astype(jnp.float32)
    clipped = jnp.clip(offset, 0, width - 1)
    column_block = lax.all_gather(vectors, "row", axis=1, tiled=True)
    picked = jnp.take(column_block, tile_cols.reshape(-1), axis=1).reshape(count, tile_count, tile)
    tile_out = jnp.einsum("trj,ktj->ktr", tile_values, picked, preferred_element_type=jnp.float32)
    block_rows = cols_n * width
    partial_value = (
        jnp.zeros((count, block_rows // tile, tile), jnp.float32).at[:, tile_rows, :].add(tile_out)
    )
    local = lax.psum_scatter(
        partial_value.reshape(count, block_rows), "col", scatter_dimension=1, tiled=True
    )
    own_values = jnp.take(vectors, clipped, axis=1).astype(jnp.float32) * inside[None, :]
    hub_values = lax.psum(own_values, ("row", "col")).astype(jnp.bfloat16)
    weights = degrees.astype(jnp.float32)
    hub_partial = lax.dot_general(
        vectors, hub_weight, (((1,), (1,)), ((), ())), preferred_element_type=jnp.float32
    )
    along_part = jnp.dot(vectors.astype(jnp.float32), weights, precision=lax.Precision.HIGHEST)
    weight_part = jnp.sum(weights)
    hubbed = local + jnp.dot(hub_values, hub_weight, preferred_element_type=jnp.float32)
    hub_sums, along, total = lax.psum((hub_partial, along_part, weight_part), ("row", "col"))
    hubbed = hubbed.at[:, clipped].add(hub_sums * inside[None, :])
    image = hubbed - (along / total)[:, None] * weights[None, :]
    gram_part = jnp.dot(image, image.T, precision=lax.Precision.HIGHEST)
    gram = lax.psum(gram_part, ("row", "col")) / jnp.float32(width * rows_n * cols_n)
    factor = jnp.linalg.cholesky(gram)
    basis = lax.linalg.triangular_solve(factor, image, left_side=True, lower=True)
    return (basis, factor)


def solution(mesh):
    in_specs = (
        P(None, ("row", "col")),
        P(("row", "col")),
        P(),
        P(None, ("row", "col")),
        P(("row", "col"), None, None),
        P(("row", "col")),
        P(("row", "col"), None),
    )
    out_specs = (P(None, ("row", "col")), P())
    return jax.shard_map(
        on_device, mesh=mesh, in_specs=in_specs, out_specs=out_specs, check_vma=False
    )
```

profile of v0, /device:TPU:1, one launch (start us, length us, event | category | flops | bytes accessed | tf_op | source)
XLA Modules:
  0.0 357.2 jit_solution(12037594014195212301)
XLA Ops:
  8.0 0.0 copy-start
  8.0 0.0 copy-start.1
  8.0 0.0 all-reduce.3.cloned.1.call-start
  8.1 2.4 fusion.14
  10.5 0.0 all-reduce.3.cloned.1.call-update
  10.5 0.0 reduce-scatter.2.cloned.1.call-start
  10.5 0.8 copy.9
  11.4 28.8 %all_gather.3 = bf16[16,8192]{0,1:T(8,128)(2,1)} all-gather(bf16[16,512]{0,1:T(8,128)(2,1)S(1)} %copy.9), channel_id=1, replica_groups=mesh['row'=16,'col'=16] {'row'}, dimensions={1}, use_global_device_ids=true | all-gather | bytes 278528 | tf_op jit(solution)/shard_map/all_gather | solution.py:18
  40.2 0.0 copy-done.1
  40.2 0.1 compare_select_fusion
  40.3 0.0 copy-start.8
  40.3 43.3 %gather_fusion = bf16[12288,16]{1,0:T(8,128)(2,1)} fusion(bf16[16,8192]{0,1:T(8,128)(2,1)} %all_gather.3, s32[12288]{0:T(1024)S(1)} %broadcast_clamp_fusion), kind=kCustom, calls=%fused_computation | custom fusion | bytes 835584 | tf_op jit(solution)/shard_map/jit(_take)/gather | solution.py:19
  83.7 3.8 %copy.10 = bf16[16,96,128]{2,0,1:T(8,128)(2,1)} copy(bf16[16,96,128]{0,2,1:T(8,128)(2,1)} %bitcast.33) | data formatting | bytes 786432 | tf_op jit(solution)/shard_map/jit(_take)/gather | solution.py:19
  87.5 0.0 copy-done.8
  87.5 0.0 copy-done
  87.5 3.6 %fusion = f32[96,16,128]{2,1,0:T(8,128)} fusion(bf16[96,128,128]{2,1,0:T(8,128)(2,1)S(1)} %copy-done, bf16[16,96,128]{2,0,1:T(8,128)(2,1)} %copy.10, pred[96,128]{1,0:T(8,128)(4,1)S(1)} %compare_and_fusion), kind=kOutput, calls=%fused_computation.8 | convolution fusion | flops 50528256 | bytes 4337664 | tf_op jit(solution)/shard_map/trj,ktj->ktr/dot_general | solution.py:20
  91.1 0.0 copy-start.7
  91.1 0.0 copy-start.2
  91.1 0.8 broadcast_in_dim.35
  92.0 12.3 %scatter_fusion = f32[16,64,128]{2,0,1:T(8,128)} fusion(f32[16,64,128]{2,0,1:T(8,128)} %broadcast_in_dim.35, s32[96]{0:T(128)S(1)} %compare_select_fusion.3, f32[96,16,128]{2,1,0:T(8,128)} %fusion), kind=kCustom, calls=%fused_computation.2 | custom fusion | flops 196608 | bytes 2359680 | tf_op jit(solution)/shard_map/scatter-add | solution.py:23
  104.2 1.9 copy_bitcast_fusion
  106.1 0.0 reduce-scatter.2.cloned.1.call-update
  106.1 0.0 copy-done.7
  106.1 0.6 compare_and_fusion.1
  106.7 0.0 copy-start.3
  106.7 0.6 copy-done.3
  107.3 0.6 broadcast_clamp_fusion.1
  107.9 3.7 %gather_fusion.1 = bf16[1024,16]{1,0:T(8,128)(2,1)S(1)} fusion(bf16[16,512]{0,1:T(8,128)(2,1)S(1)} %copy.9, s32[1024]{0:T(1024)} %broadcast_clamp_fusion.1), kind=kCustom, calls=%fused_computation.1 | custom fusion | bytes 69632 | tf_op jit(solution)/shard_map/jit(_take)/gather | solution.py:28
  111.6 0.7 convert_element_type.16
  112.3 0.0 copy-start.5
  112.3 1.3 convert_reduce_fusion
  113.6 0.0 copy-done.2
  113.6 0.1 convolution_bitcast_fusion
  113.7 0.0 copy-done.5
  113.7 0.0 copy-start.4
  113.7 0.0 copy-start.6
  113.7 1.8 multiply_bitcast_fusion
  115.6 78.9 %all-reduce = (bf16[16,1024]{0,1:T(8,128)(2,1)S(1)}, f32[16]{0:T(128)S(1)}, f32[]{:T(128)}) all-reduce(f32[16,1024]{0,1:T(8,128)} %multiply_bitcast_fusion, f32[16]{0:T(128)S(1)} %convolution_bitcast_fusion, f32[]{:T(128)} %convert_reduce_fusion), channel_id=1, replica_groups=mesh['row'=16,'col'=16] {'row','col'}, use_global_device_ids=true, to_apply=%region_2.3 | all-reduce | flops 16401 | bytes 98440 | tf_op jit(solution)/shard_map/psum | solution.py:29
  194.5 0.6 broadcast_divide_fusion
  195.1 62.1 %all-reduce.3.cloned.1.call-done = f32[16,1024]{1,0:T(8,128)} async-done(((f32[16,1024]{1,0:T(8,128)}), f32[16,1024]{1,0:T(8,128)}) %all-reduce.3.cloned.1.call-update) | async-done | bytes 65552 | tf_op jit(solution)/shard_map/psum | solution.py:37
  257.2 0.8 multiply_bitcast_fusion.1
  258.1 1.0 copy.14
  259.1 0.0 reduce-scatter.2.cloned.1.call-done
  259.1 1.5 convolution_add_fusion
  260.6 0.1 copy.13
  260.7 0.0 copy-done.4
  260.7 8.1 %scatter_fusion.1 = f32[16,512]{0,1:T(8,128)S(1)} fusion(f32[16,512]{0,1:T(8,128)S(1)} %copy.13, s32[1024]{0:T(1024)S(1)} %copy-done.4, f32[1024,16]{1,0:T(8,128)} %copy.14), kind=kCustom, calls=%fused_computation.3 | custom fusion | flops 16384 | bytes 200704 | tf_op jit(solution)/shard_map/scatter-add | solution.py:38
  268.9 0.0 copy-done.6
  268.9 0.7 fusion.5
  269.6 74.4 %psum.39 = f32[16,16]{0,1:T(8,128)S(1)} all-reduce(f32[16,16]{0,1:T(8,128)S(1)} %fusion.5), channel_id=1, replica_groups=mesh['row'=16,'col'=16] {'row','col'}, use_global_device_ids=true, to_apply=%region_8.9 | all-reduce | flops 256 | bytes 2048 | tf_op jit(solution)/shard_map/psum | solution.py:41
  344.0 0.1 copy.16
  344.1 1.5 cholesky.16
  345.6 0.6 compare_reduce_fusion
  346.2 1.2 select_bitcast_fusion
  347.5 1.2 custom-call.6
  348.7 1.1 fusion.4
  (6 shorter events, 0.1 us)
Async XLA Ops:
  8.0 79.5 %copy-start = (bf16[96,128,128]{2,1,0:T(8,128)(2,1)S(1)}, bf16[96,128,128]{2,1,0:T(8,128)(2,1)}, u32[]{:S(2)}) copy-start(bf16[96,128,128]{2,1,0:T(8,128)(2,1)} %param.11) | copy-start | bytes 9437188
  8.0 32.2 %copy-start.1 = (s32[96,128]{1,0:T(8,128)S(1)}, s32[96,128]{1,0:T(8,128)}, u32[]{:S(2)}) copy-start(s32[96,128]{1,0:T(8,128)} %param.13) | copy-start | bytes 147460
  8.0 249.2 %all-reduce.3.cloned.1.call-start = ((), (), s32[]{:S(2)}) async-start(), calls=%async_computation.2 | async-start | bytes 131072 | tf_op jit(solution)/shard_map/psum | solution.py:37
  10.5 248.6 %reduce-scatter.2.cloned.1.call-start = ((), (), s32[]{:S(2)}) async-start(), calls=%async_computation.1 | async-start | bytes 557056 | tf_op jit(solution)/shard_map/reduce_scatter | solution.py:25
  40.3 47.2 %copy-start.8 = (s32[96]{0:T(128)S(1)}, s32[96]{0:T(128)}, u32[]{:S(2)}) copy-start(s32[96]{0:T(128)} %param.12) | copy-start | bytes 1156
  91.1 15.0 %copy-start.7 = (s32[1024]{0:T(1024)S(1)}, s32[1024]{0:T(1024)}, u32[]{:S(2)}) copy-start(s32[1024]{0:T(1024)} %param.9) | copy-start | bytes 12292
  91.1 22.4 %copy-start.2 = (bf16[16,512]{1,0:T(8,128)(2,1)S(1)}, bf16[16,512]{1,0:T(8,128)(2,1)}, u32[]{:S(2)}) copy-start(bf16[16,512]{1,0:T(8,128)(2,1)} %param.7) | copy-start | bytes 49156
  106.7 0.6 copy-start.3
  112.3 1.4 copy-start.5
  113.7 147.0 %copy-start.4 = (s32[1024]{0:T(1024)S(1)}, s32[1024]{0:T(1024)}, u32[]{:S(2)}) copy-start(s32[1024]{0:T(1024)} %copy-done.3) | copy-start | bytes 12292
  113.7 155.2 %copy-start.6 = (f32[512]{0:T(512)S(1)}, f32[512]{0:T(512)}, u32[]{:S(2)}) copy-start(f32[512]{0:T(512)} %copy-done.5) | copy-start | bytes 6148
Sparse Core Ops, SparseCore 0:
  15.3 241.9 all-reduce.2
Sparse Core Ops, SparseCore 1:
  106.2 73.2 reduce-scatter.1
where the time goes:
time: 358 us; the launch traced here: 357 us
  blocking collectives  182 us (51%)
  waiting for transfers between devices  62.2 us (17%)
  local copies, waits for them, and re-layouts  56.3 us (16%)
  other arithmetic  31.5 us (9%)
  between operations  15.6 us (4%)
  matrix products  9.4 us (3%)
    psum x1, blocking collectives, on_device(): hub_values = lax.psum(own_values, ('row', 'col')).astype(jnp.bfloat16)  78.9 us
    psum x1, blocking collectives, on_device(): lax.psum(gram_part, ('row', 'col')) / jnp.float32(width * rows_n * cols_n)  74.4 us
    psum x1, waiting for transfers between devices, on_device(): lax.psum((hub_partial, along_part, weight_part), ('row', 'col'))  62.1 us
    gather x2, local copies, waits for them, and re-layouts, on_device(): jnp.take(column_block, tile_cols.reshape(-1), axis=1)  47.2 us
    all_gather x1, blocking collectives, on_device(): column_block = lax.all_gather(vectors, 'row', axis=1, tiled=True)  28.8 us
    scatter-add x1, other arithmetic, on_device(): jnp.zeros((count, block_rows // tile, tile), jnp.float32)  12.3 us
    scatter-add x1, other arithmetic, on_device(): hubbed = hubbed.at[:, clipped].add(hub_sums * inside[None, :])  8.13 us
  transfers between devices with their start and end apart: 2, of which 1 were waited for; matrix products, arithmetic and copies ran while one was open for 22% of the time, Pallas kernels for 0%

commit v1 on v0

v1 whole, which is shorter than its diff:
```python
import functools

import jax
import jax.numpy as jnp
from jax import lax
from jax.experimental import pallas as pl
from jax.experimental.pallas import tpu as pltpu
from jax.sharding import PartitionSpec as P

f32, bf16, i32 = jnp.float32, jnp.bfloat16, jnp.int32
MIB = 2**20
LANES = 128


def dot_t(a, b, precision=None):
    return lax.dot_general(
        a, b, (((1,), (1,)), ((), ())), precision=precision, preferred_element_type=f32
    )


def lane_of(rows, width=LANES):
    return lax.broadcasted_iota(i32, (rows, width), 1)


def lane_sum(a):
    return jnp.sum(a, axis=1, keepdims=True)


def pieces(a, count):
    found = []
    for _ in range(count):
        head = a.astype(bf16).astype(f32)
        found.append(head)
        a = a - head
    return found


def prepare(ids, x_ref, degree_ref, weight_ref, out_ref):
    i, j = lax.axis_index("row"), lax.axis_index("col")
    piece = i * lax.axis_size("col") + j
    peers, _, count, _ = out_ref.shape
    x = x_ref[...]
    wide = x.astype(f32)
    width = x.shape[1]
    own = ids.shape[0] // (peers * lax.axis_size("col"))
    lane = lane_of(count)
    place = lane_of(count, width)
    degrees = degree_ref[...].astype(f32)
    along = jnp.zeros((count, LANES), f32)
    for r in range(width // LANES):
        along += wide[:, r * LANES : (r + 1) * LANES] * degrees[r : r + 1]
    along = lane_sum(along)
    total = lane_sum(jnp.sum(degrees, axis=0, keepdims=True))
    extra = jnp.zeros((count, LANES), f32)
    for k in range(own):
        offset = ids[piece * own + k] - piece * width
        value = lane_sum(jnp.where(place == offset, wide, 0.0))
        extra = jnp.where(lane == i * own + k, value, extra)
    for at, value in enumerate(pieces(along, 3) + pieces(total, 2)):
        extra = jnp.where(lane == 64 + at, value, extra)
    extra = extra.astype(bf16)
    part = dot_t(x, weight_ref[...])
    for m in range(peers // 2):
        head, tail = pieces(part[:, m * LANES : (m + 1) * LANES], 2)
        even = jnp.where(lane < 64, head, pltpu.roll(tail, 64, 1))
        odd = jnp.where(lane < 64, pltpu.roll(head, 64, 1), tail)
        out_ref[2 * m, 4] = even.astype(bf16)
        out_ref[2 * m + 1, 4] = odd.astype(bf16)
    for s in range(peers):
        for r in range(4):
            out_ref[s, r] = x[:, r * LANES : (r + 1) * LANES]
        out_ref[s, 5] = extra


def tiles(rows, cols_ref, got_ref, value_ref, out_ref, table, picked):
    peers, _, count, _ = out_ref.shape
    tile_count = cols_ref.shape[0]
    lane = lane_of(count)
    for s in range(peers):
        for a in range(2):
            at = pl.ds((s * 2 + a) * count, count)
            table[at, 0:LANES] = got_ref[s, 2 * a]
            table[at, LANES : 2 * LANES] = got_ref[s, 2 * a + 1]
    for s in range(peers):
        for r in range(4):
            out_ref[s, r] = jnp.zeros((count, LANES), f32)
    sums = jnp.zeros((count, LANES), f32)
    extra = jnp.zeros((count, LANES), f32)
    for s in range(got_ref.shape[0]):
        sums += got_ref[s, 4].astype(f32)
        extra += got_ref[s, 5].astype(f32)
    along = lane_sum(jnp.where((lane >= 64) & (lane < 67), extra, 0.0))
    total = lane_sum(jnp.where((lane >= 67) & (lane < 69), extra, 0.0))
    base = jnp.where(lane < 64, extra, sums + pltpu.roll(sums, 64, 1))
    for s in range(peers):
        block = jnp.where(lane == 64 + (4 * s + 4) % 64, along, base)
        out_ref[s, 4] = jnp.where(lane == 64 + (4 * s + 5) % 64, total, block)

    def pick(p):
        hot, high = [], []
        for e in range(2):
            at = cols_ref[pl.ds(2 * p + e, 1), :]
            high.append(jnp.broadcast_to(at >> 8, (8, LANES)))
            low = (at & 255).astype(jnp.int16)
            place = lax.broadcasted_iota(jnp.int16, (2 * LANES, LANES), 0)
            hot.append(jnp.where(place == low, jnp.ones((), bf16), jnp.zeros((), bf16)))
        found = jnp.dot(table[...], jnp.concatenate(hot, 1), preferred_element_type=f32)
        for e in range(2):
            top = jnp.zeros((8, LANES), f32)
            low = jnp.zeros((8, LANES), f32)
            for h in range(2 * peers):
                mask = high[e] == h
                columns = slice(e * LANES, (e + 1) * LANES)
                top = jnp.where(mask, found[h * 16 : h * 16 + 8, columns], top)
                low = jnp.where(mask, found[h * 16 + 8 : h * 16 + 16, columns], low)
            picked[2 * p + e] = jnp.concatenate([top, low], 0).astype(bf16)

    def pick_some(n, carry):
        for u in range(6):
            pick(n * 6 + u)
        return carry

    lax.fori_loop(0, tile_count // 12, pick_some, 0)

    def multiply(n, carry):
        made = [dot_t(picked[n * 16 + u], value_ref[n * 16 + u]) for u in range(16)]
        for u in range(16):
            row = rows[n * 16 + u]
            out_ref[row >> 2, row & 3] += made[u]
        return carry

    lax.fori_loop(0, tile_count // 16, multiply, 0)


def correct(ids, got_ref, degree_ref, weight_ref, image_ref, out_ref):
    i, j = lax.axis_index("row"), lax.axis_index("col")
    piece = i * lax.axis_size("col") + j
    peers, _, count, _ = got_ref.shape
    width = degree_ref.shape[0] * LANES
    own = ids.shape[0] // (peers * lax.axis_size("row"))
    lane = lane_of(count)
    half = lane_of(8)
    source = (half & 63) >> 2
    blocks = []
    for r in range(5):
        total = got_ref[0, r]
        for s in range(1, peers):
            total += got_ref[s, r]
        blocks.append(total)
    extra = blocks[4]
    pick = lambda at: lane_sum(jnp.where(lane == at, extra, 0.0))
    ratio = pick(64 + ((4 * j + 4) & 63)) / pick(64 + ((4 * j + 5) & 63))
    values = []
    for m in range(ids.shape[0] // LANES):
        at = 8 * m + 4 * (half >> 6) + (half & 3)
        parts = []
        for q in range(2):
            found = jnp.zeros((8, LANES), f32)
            for s in range(peers):
                moved = jnp.take_along_axis(got_ref[s, 4, 8 * q : 8 * q + 8], at, axis=1)
                found = jnp.where(source == s, moved, found)
            parts.append(found)
        values.append(jnp.concatenate(parts, 0).astype(bf16))
    hub = jnp.dot(jnp.concatenate(values, 1), weight_ref[...], preferred_element_type=f32)
    degrees = degree_ref[...].astype(f32)
    hub_at = [ids[piece * own + k] - piece * width for k in range(own)]
    hub_sum = [pick(64 + 4 * j + k) for k in range(own)]
    for r in range(width // LANES):
        block = blocks[r] + hub[:, r * LANES : (r + 1) * LANES]
        for k in range(own):
            block += jnp.where(lane + r * LANES == hub_at[k], hub_sum[k], 0.0)
        image_ref[:, r * LANES : (r + 1) * LANES] = block - ratio * degrees[r : r + 1]
    image = image_ref[...]
    gram = dot_t(image, image, lax.Precision.HIGHEST)
    packed = jnp.concatenate([gram[0:8], gram[8:16], jnp.zeros((8, LANES - 32), f32)], 1)
    for s in range(out_ref.shape[0]):
        out_ref[s] = packed


def add_up(got_ref, out_ref):
    total = got_ref[0]
    for s in range(1, got_ref.shape[0]):
        total += got_ref[s]
    for s in range(out_ref.shape[0]):
        out_ref[s] = total


def finish(scale, got_ref, image_ref, basis_ref, factor_ref):
    total = got_ref[0]
    for s in range(1, got_ref.shape[0]):
        total += got_ref[s]
    total = total * scale
    count, width = image_ref.shape
    left = jnp.concatenate([total, pltpu.roll(total, LANES - 16, 1)], 0)
    image = image_ref[...]
    lane = lane_of(count)
    row = lax.broadcasted_iota(i32, (count, LANES), 0)
    wide_row = lax.broadcasted_iota(i32, (count, width), 0)
    factor = jnp.zeros((count, LANES), f32)
    for k in range(count):
        column = left[:, k : k + 1]
        root = jnp.sqrt(column[k : k + 1])
        inverse = 1.0 / root
        column = column * inverse
        factor = jnp.where((lane == k) & (row >= k), column, factor)
        left = left - column * (left[k : k + 1] * inverse)
        solved = image[k : k + 1] * inverse
        image = jnp.where(
            wide_row == k, solved, jnp.where(wide_row > k, image - column * solved, image)
        )
    basis_ref[...] = image
    factor_ref[...] = factor[:, 0:count]


def on_device(vectors, degrees, hub_ids, hub_weight, tile_values, tile_rows, tile_cols):
    count, width = vectors.shape
    rows_n, cols_n = lax.axis_size("row"), lax.axis_size("col")
    smem = pl.BlockSpec(memory_space=pltpu.SMEM)
    vmem = pl.BlockSpec(memory_space=pltpu.VMEM)
    shape = jax.ShapeDtypeStruct
    degree_rows = degrees.reshape(width // LANES, LANES)

    def call(body, out, ins, limit, name, scratch=()):
        return pl.pallas_call(
            body,
            out_shape=out,
            in_specs=ins,
            out_specs=jax.tree.map(lambda _: vmem, out),
            scratch_shapes=scratch,
            compiler_params=pltpu.CompilerParams(vmem_limit_bytes=limit * MIB),
            name=name,
        )

    sent = call(
        prepare, shape((rows_n, 6, count, LANES), bf16), [smem, vmem, vmem, vmem], 8, "prepare"
    )(hub_ids, vectors, degree_rows, hub_weight)
    got = lax.all_to_all(sent, "row", 0, 0)
    sent = call(
        tiles,
        shape((cols_n, 5, count, LANES), f32),
        [smem, vmem, vmem, vmem],
        24,
        "tiles",
        [
            pltpu.VMEM((2 * rows_n * count, 2 * LANES), bf16),
            pltpu.VMEM((tile_values.shape[0], count, LANES), bf16),
        ],
    )(tile_rows, tile_cols, got, tile_values)
    got = lax.all_to_all(sent, "col", 0, 0)
    image, sent = call(
        correct,
        (shape((count, width), f32), shape((rows_n, 8, LANES), f32)),
        [smem, vmem, vmem, vmem],
        8,
        "correct",
    )(hub_ids, got, degree_rows, hub_weight)
    got = lax.all_to_all(sent, "row", 0, 0)
    sent = call(add_up, shape((cols_n, 8, LANES), f32), [vmem], 4, "add_up")(got)
    got = lax.all_to_all(sent, "col", 0, 0)
    return call(
        functools.partial(finish, 1.0 / (width * rows_n * cols_n)),
        (shape((count, width), f32), shape((count, count), f32)),
        [vmem, vmem],
        4,
        "finish",
    )(got, image)


def solution(mesh):
    in_specs = (
        P(None, ("row", "col")),
        P(("row", "col")),
        P(),
        P(None, ("row", "col")),
        P(("row", "col"), None, None),
        P(("row", "col")),
        P(("row", "col"), None),
    )
    out_specs = (P(None, ("row", "col")), P())
    return jax.shard_map(
        on_device, mesh=mesh, in_specs=in_specs, out_specs=out_specs, check_vma=False
    )
```

time: 358 us -> 84.5 us (0.24)
  blocking collectives: 182 us -> 64.7 us
  waiting for transfers between devices: 62.2 us -> 0 us
  local copies, waits for them, and re-layouts: 56.3 us -> 6.66 us
  other arithmetic: 31.5 us -> 0 us
  between operations: 15.6 us -> 0.67 us
  Pallas kernels: 0 us -> 12 us
  matrix products: 9.4 us -> 0 us
    psum x2 -> x0, blocking collectives: 153 us -> none  [the longest x1 78.9 us: on_device(): hub_values = lax.psum(own_values, ('row', 'col')).astype(jnp.bfloat16)]
    all_to_all x0 -> x4, blocking collectives: none -> 64.7 us  [the longest x2 35.2 us: on_device(): got = lax.all_to_all(sent, 'row', 0, 0)]
    psum x1 -> x0, waiting for transfers between devices: 62.1 us -> none  [on_device(): lax.psum((hub_partial, along_part, weight_part), ('row', 'col'))]
    gather x3 -> x0, local copies, waits for them, and re-layouts: 50.9 us -> none  [the longest x2 47.2 us: on_device(): jnp.take(column_block, tile_cols.reshape(-1), axis=1)]
    all_gather x1 -> x0, blocking collectives: 28.8 us -> none  [on_device(): column_block = lax.all_gather(vectors, 'row', axis=1, tiled=True)]
    scatter-add x2 -> x0, other arithmetic: 20.4 us -> none  [the longest x1 12.3 us: on_device(): jnp.zeros((count, block_rows // tile, tile), jnp.float32)]
    pallas_call x0 -> x5, Pallas kernels: none -> 12 us  [the longest x1 7.67 us: on_device(): call(tiles, shape((cols_n, 5, count, LANES), f32), [smem, vmem, vmem, vme...]
    dot_general x5 -> x0, matrix products: 8.33 us -> none  [the longest x1 3.62 us: on_device(): jnp.einsum('trj,ktj->ktr', tile_values, picked, preferred_element_type=jn...]
  transfers between devices with their start and end apart: 2 -> 0, of which waited for: 1 -> 0; matrix products, arithmetic and copies ran while one was open for 22% -> 0% of each run, Pallas kernels for 0% -> 0%
where the time goes in v1:
time: 84.5 us; the launch traced here: 84 us
  blocking collectives  64.7 us (77%)
  Pallas kernels  12 us (14%)
  local copies, waits for them, and re-layouts  6.66 us (8%)
    all_to_all x2, blocking collectives, on_device(): got = lax.all_to_all(sent, 'row', 0, 0)  35.2 us
    all_to_all x2, blocking collectives, on_device(): got = lax.all_to_all(sent, 'col', 0, 0)  29.5 us
    pallas_call x1, Pallas kernels, on_device(): call(tiles, shape((cols_n, 5, count, LANES), f32), [smem, vmem, vmem, vme...  7.67 us
    unnamed x20, local copies, waits for them, and re-layouts  6.66 us
    pallas_call x1, Pallas kernels, on_device(): call(functools.partial(finish, 1.0 / (width * rows_n * cols_n)), (shape((...  2 us

profile of v1, /device:TPU:1, one launch (start us, length us, event | category | flops | bytes accessed | tf_op | source)
XLA Modules:
  0.0 84.0 jit_solution(10816910473204978378)
XLA Ops:
  0.6 0.0 copy-start
  0.6 1.2 %copy-done = bf16[1024,512]{1,0:T(8,128)(2,1)S(1)} copy-done((bf16[1024,512]{1,0:T(8,128)(2,1)S(1)}, bf16[1024,512]{1,0:T(8,128)(2,1)}, u32[]{:S(2)}) %copy-start) | copy-done | bytes 1048600
  1.9 0.0 copy-start.4
  1.9 0.7 copy-done.4
  2.6 0.0 copy-start.5
  2.6 0.7 copy-done.5
  3.3 0.0 copy-start.7
  3.3 0.7 copy-done.7
  3.9 1.1 %prepare.1 = bf16[16,6,16,128]{3,2,1,0:T(8,128)(2,1)S(1)} custom-call(s32[1024]{0:T(1024)S(1)} %copy-done.5, bf16[16,512]{1,0:T(8,128)(2,1)S(1)} %copy-done.4, s32[4,128]{1,0:T(4,128)S(1)} %bitcast.1, bf16[1024,512]{1,0:T(8,128)(2,1)S(1)} %copy-done), custom_call_target="tpu_custom_call" | custom-call | tf_op jit(solution)/shard_map/prepare/pallas_call | solution.py:234
  5.0 0.0 copy-start.1
  5.0 24.5 %all_to_all.20.got_ref = bf16[16,6,16,128]{3,2,1,0:T(8,128)(2,1)S(1)} all-to-all(bf16[16,6,16,128]{3,2,1,0:T(8,128)(2,1)S(1)} %prepare.1), channel_id=1, replica_groups=mesh['row'=16,'col'=16] {'row'}, dimensions={0} | all-to-all | bytes 786432 | tf_op jit(solution)/shard_map/all_to_all | solution.py:237
  29.5 0.0 copy-start.2
  29.5 1.9 %copy-done.2 = bf16[96,128,128]{2,1,0:T(8,128)(2,1)S(1)} copy-done((bf16[96,128,128]{2,1,0:T(8,128)(2,1)S(1)}, bf16[96,128,128]{2,1,0:T(8,128)(2,1)}, u32[]{:S(2)}) %copy-start.2) | copy-done | bytes 3145752
  31.4 0.0 copy-start.3
  31.4 0.8 copy-done.3
  32.2 0.0 copy-start.9
  32.2 0.7 copy-done.9
  32.8 0.0 copy-start.6
  32.8 0.0 copy-start.8
  32.8 7.7 %tiles.1 = f32[16,5,16,128]{3,2,1,0:T(8,128)S(1)} custom-call(s32[96]{0:T(128)S(1)} %copy-done.9, s32[96,128]{1,0:T(8,128)S(1)} %copy-done.3, bf16[16,6,16,128]{3,2,1,0:T(8,128)(2,1)S(1)} %all_to_all.20.got_ref, bf16[96,128,128]{2,1,0:T(8,128)(2,1)S(1)} %copy-done.2), custom_call_target="tpu_custom_call" | custom-call | tf_op jit(solution)/shard_map/tiles/pallas_call | solution.py:238
  40.5 20.4 %all_to_all.21.got_ref = f32[16,5,16,128]{3,2,1,0:T(8,128)S(1)} all-to-all(f32[16,5,16,128]{3,2,1,0:T(8,128)S(1)} %tiles.1), channel_id=1, replica_groups=mesh['row'=16,'col'=16] {'col'}, dimensions={0} | all-to-all | bytes 1310720 | tf_op jit(solution)/shard_map/all_to_all | solution.py:249
  60.9 0.0 copy-done.1
  60.9 0.0 copy-done.6
  60.9 0.0 copy-done.8
  60.9 1.3 %correct.1 = (f32[16,512]{1,0:T(8,128)S(1)}, f32[16,8,128]{2,1,0:T(8,128)S(1)}) custom-call(s32[1024]{0:T(1024)S(1)} %copy-done.6, f32[16,5,16,128]{3,2,1,0:T(8,128)S(1)} %all_to_all.21.got_ref, s32[4,128]{1,0:T(4,128)S(1)} %bitcast.2, bf16[1024,512]{1,0:T(8,128)(2,1)S(1)} %copy-done.1), custom_call_target="tpu_custom_call" | custom-call | tf_op jit(solution)/shard_map/correct/pallas_call | solution.py:250
  62.2 10.7 %all_to_all.22.got_ref = f32[16,8,128]{2,1,0:T(8,128)S(1)} all-to-all(f32[16,8,128]{2,1,0:T(8,128)S(1)} %get-tuple-element.4), channel_id=1, replica_groups=mesh['row'=16,'col'=16] {'row'}, dimensions={0} | all-to-all | bytes 131072 | tf_op jit(solution)/shard_map/all_to_all | solution.py:257
  72.9 9.1 %all_to_all.23.got_ref = f32[16,8,128]{2,1,0:T(8,128)S(1)} all-to-all(f32[16,8,128]{2,1,0:T(8,128)S(1)} %add_up.1), channel_id=1, replica_groups=mesh['row'=16,'col'=16] {'col'}, dimensions={0} | all-to-all | bytes 131072 | tf_op jit(solution)/shard_map/all_to_all | solution.py:259
  82.0 2.0 %finish.1 = (f32[16,512]{1,0:T(8,128)}, f32[16,16]{1,0:T(8,128)}) custom-call(f32[16,8,128]{2,1,0:T(8,128)S(1)} %all_to_all.23.got_ref, f32[16,512]{1,0:T(8,128)S(1)} %get-tuple-element.5.image_ref), custom_call_target="tpu_custom_call" | custom-call | tf_op jit(solution)/shard_map/finish/pallas_call | solution.py:260
  (1 shorter events, 0.0 us)
Async XLA Ops:
  0.6 1.2 %copy-start = (bf16[1024,512]{1,0:T(8,128)(2,1)S(1)}, bf16[1024,512]{1,0:T(8,128)(2,1)}, u32[]{:S(2)}) copy-start(bf16[1024,512]{1,0:T(8,128)(2,1)} %weight_ref.3) | copy-start | bytes 3145732
  1.9 0.7 copy-start.4
  2.6 0.7 copy-start.5
  3.3 0.7 copy-start.7
  5.0 55.9 %copy-start.1 = (bf16[1024,512]{1,0:T(8,128)(2,1)S(1)}, bf16[1024,512]{1,0:T(8,128)(2,1)}, u32[]{:S(2)}) copy-start(bf16[1024,512]{1,0:T(8,128)(2,1)} %weight_ref.3) | copy-start | bytes 3145732
  29.5 1.9 %copy-start.2 = (bf16[96,128,128]{2,1,0:T(8,128)(2,1)S(1)}, bf16[96,128,128]{2,1,0:T(8,128)(2,1)}, u32[]{:S(2)}) copy-start(bf16[96,128,128]{2,1,0:T(8,128)(2,1)} %value_ref.1) | copy-start | bytes 9437188
  31.4 0.8 copy-start.3
  32.2 0.7 copy-start.9
  32.8 28.1 %copy-start.6 = (s32[1024]{0:T(1024)S(1)}, s32[1024]{0:T(1024)}, u32[]{:S(2)}) copy-start(s32[1024]{0:T(1024)} %ids.3) | copy-start | bytes 12292
  32.8 28.1 %copy-start.8 = (s32[512]{0:T(512)S(1)}, s32[512]{0:T(512)}, u32[]{:S(2)}) copy-start(s32[512]{0:T(512)} %param.8) | copy-start | bytes 6148

commit v2 on v1

v2 whole, which is shorter than its diff:
```python
import functools

import jax
import jax.numpy as jnp
from jax import lax
from jax.experimental import pallas as pl
from jax.experimental.pallas import tpu as pltpu
from jax.sharding import Mesh
from jax.sharding import PartitionSpec as P

f32, bf16, i32 = jnp.float32, jnp.bfloat16, jnp.int32
MIB = 2**20
LANES = 128


def dot_t(a, b, precision=None):
    return lax.dot_general(
        a, b, (((1,), (1,)), ((), ())), precision=precision, preferred_element_type=f32
    )


def lane_of(rows, width=LANES):
    return lax.broadcasted_iota(i32, (rows, width), 1)


def lane_sum(a):
    return jnp.sum(a, axis=1, keepdims=True)


def pieces(a, count):
    found = []
    for _ in range(count):
        head = a.astype(bf16).astype(f32)
        found.append(head)
        a = a - head
    return found


def prepare(
    ids_hbm, x_hbm, degree_hbm, weight_hbm, out_ref, ids, x_ref, degree_ref, weight_ref, done
):
    pairs = ((weight_hbm, weight_ref), (x_hbm, x_ref), (degree_hbm, degree_ref), (ids_hbm, ids))
    copies = [pltpu.make_async_copy(a, b, done.at[n]) for n, (a, b) in enumerate(pairs)]
    for copy in copies:
        copy.start()
    row = lax.axis_index("z") * 2 + lax.axis_index("core")
    piece = row * lax.axis_size("col") + lax.axis_index("col")
    peers, _, count, _ = out_ref.shape
    width = x_ref.shape[1]
    own = ids.shape[0] // (2 * peers * lax.axis_size("col"))
    lane = lane_of(count)
    place = lane_of(count, width)
    for copy in copies[1:]:
        copy.wait()
    x = x_ref[...]
    wide = x.astype(f32)
    degrees = degree_ref[...].astype(f32)
    along = jnp.zeros((count, LANES), f32)
    for r in range(width // LANES):
        along += wide[:, r * LANES : (r + 1) * LANES] * degrees[r : r + 1]
    along = lane_sum(along)
    total = lane_sum(jnp.sum(degrees, axis=0, keepdims=True))
    extra = jnp.zeros((count, LANES), f32)
    for k in range(own):
        offset = ids[piece * own + k] - piece * width
        value = lane_sum(jnp.where(place == offset, wide, 0.0))
        extra = jnp.where(lane == row * own + k, value, extra)
    for at, value in enumerate(pieces(along, 3) + pieces(total, 2)):
        extra = jnp.where(lane == 64 + at, value, extra)
    extra = extra.astype(bf16)
    for s in range(peers):
        for r in range(4):
            out_ref[s, r] = x[:, r * LANES : (r + 1) * LANES]
        out_ref[s, 6] = extra
    copies[0].wait()
    part = dot_t(x, weight_ref[...])
    for s in range(peers):
        head, tail = pieces(part[:, s * LANES : (s + 1) * LANES], 2)
        even = jnp.where(lane < 64, head, pltpu.roll(tail, 64, 1))
        odd = jnp.where(lane < 64, pltpu.roll(head, 64, 1), tail)
        out_ref[s, 4] = even.astype(bf16)
        out_ref[s, 5] = odd.astype(bf16)


def tiles(
    rows_hbm,
    cols_hbm,
    near_ref,
    far_ref,
    value_hbm,
    out_ref,
    rows,
    cols_ref,
    value_ref,
    table,
    blocks,
    picked,
    done,
):
    pairs = ((cols_hbm, cols_ref), (rows_hbm, rows), (value_hbm, value_ref))
    copies = [pltpu.make_async_copy(a, b, done.at[n]) for n, (a, b) in enumerate(pairs)]
    for copy in copies:
        copy.start()
    peers, _, count, _ = out_ref.shape
    tile_count = cols_ref.shape[0]
    core = lax.axis_index("core")
    lane = lane_of(count)
    sums = jnp.zeros((count, LANES), f32)
    extra = jnp.zeros((count, LANES), f32)
    for side, got_ref in ((core, near_ref), (1 - core, far_ref)):
        for z in range(got_ref.shape[0]):
            for r in range(4):
                block = got_ref[z, r]
                at = pl.multiple_of((z * 4 + side * 2 + r // 2) * count, count)
                table[pl.ds(at, count), (r % 2) * LANES : (r % 2 + 1) * LANES] = block
                blocks[z * 8 + side * 4 + r] = block.astype(f32)
            sums += got_ref[z, 4 + core].astype(f32)
            extra += got_ref[z, 6].astype(f32)
    along = lane_sum(jnp.where((lane >= 64) & (lane < 67), extra, 0.0))
    total = lane_sum(jnp.where((lane >= 67) & (lane < 69), extra, 0.0))
    base = jnp.where(lane < 64, extra, sums + pltpu.roll(sums, 64, 1))
    for s in range(peers):
        for r in range(4):
            out_ref[s, r] = jnp.zeros((count, LANES), f32)
        block = jnp.where(lane == 64 + (4 * s + 4) % 64, along, base)
        out_ref[s, 4] = jnp.where(lane == 64 + (4 * s + 5) % 64, total, block)

    def pick_two(t):
        hot, high, made = [], [], []
        for e in range(2):
            at = cols_ref[pl.ds(t + e, 1), :]
            high.append(jnp.broadcast_to(at >> 8, (8, LANES)))
            low = (at & 255).astype(jnp.int16)
            place = lax.broadcasted_iota(jnp.int16, (2 * LANES, LANES), 0)
            hot.append(jnp.where(place == low, jnp.ones((), bf16), jnp.zeros((), bf16)))
        found = jnp.dot(table[...], jnp.concatenate(hot, 1), preferred_element_type=f32)
        for e in range(2):
            halves = [jnp.zeros((8, LANES), f32)] * 2
            for h in range(table.shape[0] // count):
                mask = high[e] == h
                for q in range(2):
                    at = h * count + q * 8
                    part = found[at : at + 8, e * LANES : (e + 1) * LANES]
                    halves[q] = jnp.where(mask, part, halves[q])
            made.append(jnp.concatenate(halves, 0).astype(bf16))
        return made

    def pick_one(t):
        at = cols_ref[pl.ds(t, 1), :]
        low = jnp.broadcast_to(at & (LANES - 1), (8, LANES))
        high = jnp.broadcast_to(at >> 7, (8, LANES))
        halves = [jnp.zeros((8, LANES), f32)] * 2
        for h in range(blocks.shape[0]):
            mask = high == h
            for q in range(2):
                part = jnp.take_along_axis(blocks[h, q * 8 : q * 8 + 8], low, axis=1)
                halves[q] = jnp.where(mask, part, halves[q])
        return jnp.concatenate(halves, 0).astype(bf16)

    twos, ones = 8, 8
    step = 2 * twos + ones

    def pick(n):
        made = []
        for u in range(twos):
            made += pick_two(n * step + 2 * u)
        for u in range(ones):
            made.append(pick_one(n * step + 2 * twos + u))
        return made

    def multiply(n):
        return [dot_t(picked[n * step + u], value_ref[n * step + u]) for u in range(step)]

    def add(n, made):
        for u in range(step):
            at = rows[n * step + u]
            out_ref[at >> 2, at & 3] += made[u]

    def keep(n, made):
        for u in range(step):
            picked[n * step + u] = made[u]

    copies[0].wait()
    keep(0, pick(0))
    copies[1].wait()
    copies[2].wait()

    def both(n, carry):
        products = multiply(n - 1)
        made = pick(n)
        add(n - 1, products)
        keep(n, made)
        return carry

    lax.fori_loop(1, tile_count // step, both, 0)
    add(tile_count // step - 1, multiply(tile_count // step - 1))


def correct(ids, got_ref, degree_ref, weight_ref, image_ref, out_ref):
    j = lax.axis_index("col")
    row = lax.axis_index("z") * 2 + lax.axis_index("core")
    piece = row * lax.axis_size("col") + j
    peers, _, count, _ = got_ref.shape
    width = degree_ref.shape[0] * LANES
    own = ids.shape[0] // (peers * out_ref.shape[0])
    lane = lane_of(count)
    half = lane_of(8)
    source = (half & 63) >> 2
    blocks = []
    for r in range(5):
        total = got_ref[0, r]
        for s in range(1, peers):
            total += got_ref[s, r]
        blocks.append(total)
    extra = blocks[4]
    pick = lambda at: lane_sum(jnp.where(lane == at, extra, 0.0))
    ratio = pick(64 + ((4 * j + 4) & 63)) / pick(64 + ((4 * j + 5) & 63))
    values = []
    for m in range(ids.shape[0] // LANES):
        at = 8 * m + 4 * (half >> 6) + (half & 3)
        parts = []
        for q in range(2):
            found = jnp.zeros((8, LANES), f32)
            for s in range(peers):
                moved = jnp.take_along_axis(got_ref[s, 4, 8 * q : 8 * q + 8], at, axis=1)
                found = jnp.where(source == s, moved, found)
            parts.append(found)
        values.append(jnp.concatenate(parts, 0).astype(bf16))
    hub = jnp.dot(jnp.concatenate(values, 1), weight_ref[...], preferred_element_type=f32)
    degrees = degree_ref[...].astype(f32)
    hub_at = [ids[piece * own + k] - piece * width for k in range(own)]
    hub_sum = [pick(64 + 4 * j + k) for k in range(own)]
    for r in range(width // LANES):
        block = blocks[r] + hub[:, r * LANES : (r + 1) * LANES]
        for k in range(own):
            block += jnp.where(lane + r * LANES == hub_at[k], hub_sum[k], 0.0)
        image_ref[:, r * LANES : (r + 1) * LANES] = block - ratio * degrees[r : r + 1]
    image = image_ref[...]
    gram = dot_t(image, image, lax.Precision.HIGHEST)
    packed = jnp.concatenate([gram[0:8], gram[8:16], jnp.zeros((8, LANES - 32), f32)], 1)
    for s in range(out_ref.shape[0]):
        out_ref[s] = packed


def add_up(got_ref, out_ref):
    total = got_ref[0]
    for s in range(1, got_ref.shape[0]):
        total += got_ref[s]
    for s in range(out_ref.shape[0]):
        out_ref[s] = total


def finish(scale, got_ref, image_ref, basis_ref, factor_ref):
    total = got_ref[0]
    for s in range(1, got_ref.shape[0]):
        total += got_ref[s]
    total = total * scale
    count, width = image_ref.shape
    left = jnp.concatenate([total, pltpu.roll(total, LANES - 16, 1)], 0)
    image = image_ref[...]
    lane = lane_of(count)
    row = lax.broadcasted_iota(i32, (count, LANES), 0)
    columns = [jnp.broadcast_to(left[:, k : k + 1], (count, LANES)) for k in range(count)]
    parts = [image[:, r * LANES : (r + 1) * LANES] for r in range(width // LANES)]
    unit = jnp.zeros((count, LANES), f32)
    by_row = jnp.ones((count, LANES), f32)
    by_lane = jnp.ones((count, LANES), f32)
    for k in range(count):
        column = columns[k]
        pivot = column[k : k + 1]
        ratio = jnp.where(row > k, column * (1.0 / pivot), 0.0)
        for m in range(k + 1, count):
            columns[m] = columns[m] - ratio * columns[m][k : k + 1]
        for r in range(len(parts)):
            parts[r] = parts[r] - ratio * parts[r][k : k + 1]
        unit = jnp.where(lane == k, jnp.where(row == k, 1.0, ratio), unit)
        by_row = jnp.where(row == k, pivot, by_row)
        by_lane = jnp.where(lane == k, pivot, by_lane)
    inverse = 1.0 / jnp.sqrt(by_row)
    for r in range(len(parts)):
        basis_ref[:, r * LANES : (r + 1) * LANES] = parts[r] * inverse
    factor_ref[...] = (unit * jnp.sqrt(by_lane))[:, 0:count]


def on_device(vectors, degrees, hub_ids, hub_weight, tile_values, tile_rows, tile_cols):
    count, width = vectors.shape
    z_n, cols_n = lax.axis_size("z"), lax.axis_size("col")
    rows_n = 2 * z_n
    tile_count = tile_values.shape[0]
    smem = pl.BlockSpec(memory_space=pltpu.SMEM)
    vmem = pl.BlockSpec(memory_space=pltpu.VMEM)
    hbm = pl.BlockSpec(memory_space=pltpu.HBM)
    shape = jax.ShapeDtypeStruct
    degree_rows = degrees.reshape(width // LANES, LANES)

    def stay(array):
        return pltpu.with_memory_space_constraint(array, pltpu.HBM)

    def call(body, out, ins, limit, name, scratch=()):
        return pl.pallas_call(
            body,
            out_shape=out,
            in_specs=ins,
            out_specs=jax.tree.map(lambda _: vmem, out),
            scratch_shapes=scratch,
            compiler_params=pltpu.CompilerParams(vmem_limit_bytes=limit * MIB),
            name=name,
        )

    sent = call(
        prepare,
        shape((z_n, 7, count, LANES), bf16),
        [hbm] * 4,
        8,
        "prepare",
        [
            pltpu.SMEM(hub_ids.shape, i32),
            pltpu.VMEM(vectors.shape, bf16),
            pltpu.VMEM(degree_rows.shape, i32),
            pltpu.VMEM(hub_weight.shape, bf16),
            pltpu.SemaphoreType.DMA((4,)),
        ],
    )(stay(hub_ids), stay(vectors), stay(degree_rows), stay(hub_weight))
    near = lax.all_to_all(sent, "z", 0, 0)
    far = lax.ppermute(near, "core", [(0, 1), (1, 0)])
    sent = call(
        tiles,
        shape((cols_n, 5, count, LANES), f32),
        [hbm, hbm, vmem, vmem, hbm],
        24,
        "tiles",
        [
            pltpu.SMEM(tile_rows.shape, i32),
            pltpu.VMEM(tile_cols.shape, i32),
            pltpu.VMEM(tile_values.shape, bf16),
            pltpu.VMEM((2 * rows_n * count, 2 * LANES), bf16),
            pltpu.VMEM((4 * rows_n, count, LANES), f32),
            pltpu.VMEM((tile_count, count, LANES), bf16),
            pltpu.SemaphoreType.DMA((3,)),
        ],
    )(stay(tile_rows), stay(tile_cols), near, far, stay(tile_values))
    got = lax.all_to_all(sent, "col", 0, 0)
    image, sent = call(
        correct,
        (shape((count, width), f32), shape((rows_n, 8, LANES), f32)),
        [smem, vmem, vmem, vmem],
        8,
        "correct",
    )(hub_ids, got, degree_rows, hub_weight)
    got = lax.all_to_all(sent, ("z", "core"), 0, 0)
    sent = call(add_up, shape((cols_n, 8, LANES), f32), [vmem], 4, "add_up")(got)
    got = lax.all_to_all(sent, "col", 0, 0)
    return call(
        functools.partial(finish, 1.0 / (width * rows_n * cols_n)),
        (shape((count, width), f32), shape((count, count), f32)),
        [vmem, vmem],
        4,
        "finish",
    )(got, image)


def solution(mesh):
    rows_n, cols_n = mesh.devices.shape
    split = Mesh(mesh.devices.reshape(rows_n // 2, 2, cols_n), ("z", "core", "col"))
    every = ("z", "core", "col")
    in_specs = (
        P(None, every),
        P(every),
        P(),
        P(None, every),
        P(every, None, None),
        P(every),
        P(every, None),
    )
    out_specs = (P(None, every), P())
    return jax.shard_map(
        on_device, mesh=split, in_specs=in_specs, out_specs=out_specs, check_vma=False
    )
```

time: 84.5 us -> 73.2 us (0.87)
  local copies, waits for them, and re-layouts: 6.66 us -> 0.02 us
  blocking collectives: 64.7 us -> 58.8 us
  starting transfers between devices: 0 us -> 2.38 us
  Pallas kernels: 12 us -> 9.91 us
  waiting for transfers between devices: 0 us -> 1.12 us
    unnamed x20 -> x6, local copies, waits for them, and re-layouts: 6.66 us -> 0.02 us
    all_to_all x2, blocking collectives: 35.2 us -> 30.8 us  [the longest x1 18.7 us: on_device(): near = lax.all_to_all(sent, 'z', 0, 0)]
    ppermute x0 -> x1, starting transfers between devices: none -> 2.38 us  [on_device(): far = lax.ppermute(near, 'core', [(0, 1), (1, 0)])]
    all_to_all x2, blocking collectives: 29.5 us -> 28 us  [on_device(): got = lax.all_to_all(sent, 'col', 0, 0)]
    ppermute x0 -> x1, waiting for transfers between devices: none -> 1.12 us  [on_device(): far = lax.ppermute(near, 'core', [(0, 1), (1, 0)])]
    pallas_call x1, Pallas kernels: 2 us -> 0.94 us  [on_device(): call(functools.partial(finish, 1.0 / (width * rows_n * cols_n)), (shape((...]
    pallas_call x2, Pallas kernels: 8.73 us -> 7.68 us  [the longest x1 5.95 us: on_device(): call(tiles, shape((cols_n, 5, count, LANES), f32), [hbm, hbm, vmem, vmem,...]
  transfers between devices with their start and end apart: 0 -> 1, of which waited for: 0 -> 1; matrix products, arithmetic and copies ran while one was open for 0% -> 0% of each run, Pallas kernels for 0% -> 0%
where the time goes in v2:
time: 73.2 us; the launch traced here: 72.9 us
  blocking collectives  58.8 us (80%)
  Pallas kernels  9.91 us (14%)
  starting transfers between devices  2.38 us (3%)
  waiting for transfers between devices  1.12 us (2%)
    all_to_all x2, blocking collectives, on_device(): got = lax.all_to_all(sent, 'col', 0, 0)  28 us
    all_to_all x1, blocking collectives, on_device(): near = lax.all_to_all(sent, 'z', 0, 0)  18.7 us
    all_to_all x1, blocking collectives, on_device(): got = lax.all_to_all(sent, ('z', 'core'), 0, 0)  12.1 us
    pallas_call x1, Pallas kernels, on_device(): call(tiles, shape((cols_n, 5, count, LANES), f32), [hbm, hbm, vmem, vmem,...  5.95 us
    ppermute x1, starting transfers between devices, on_device(): far = lax.ppermute(near, 'core', [(0, 1), (1, 0)])  2.38 us
    pallas_call x1, Pallas kernels, on_device(): call(prepare, shape((z_n, 7, count, LANES), bf16), [hbm] * 4, 8, 'prepare...  1.73 us
  transfers between devices with their start and end apart: 1, of which 1 were waited for; matrix products, arithmetic and copies ran while one was open for 0% of the time, Pallas kernels for 0%

profile of v2, /device:TPU:1, one launch (start us, length us, event | category | flops | bytes accessed | tf_op | source)
XLA Modules:
  0.0 72.9 jit_solution(12568303044886376270)
XLA Ops:
  0.6 1.7 %prepare.1 = bf16[8,7,16,128]{3,2,1,0:T(8,128)(2,1)S(1)} custom-call(s32[1024]{0:T(1024)} %ids.1, bf16[16,512]{1,0:T(8,128)(2,1)} %x_hbm.1, s32[4,128]{1,0:T(4,128)} %bitcast.1, bf16[1024,512]{1,0:T(8,128)(2,1)} %weight_ref.1), custom_call_target="tpu_custom_call" | custom-call | tf_op jit(solution)/shard_map/prepare/pallas_call | solution.py:310
  2.4 0.0 copy-start
  2.4 0.0 copy-start.1
  2.4 0.0 copy-start.2
  2.4 18.7 %all_to_all.20.near_ref = bf16[8,7,16,128]{3,2,1,0:T(8,128)(2,1)S(1)} all-to-all(bf16[8,7,16,128]{3,2,1,0:T(8,128)(2,1)S(1)} %prepare.1), channel_id=1, replica_groups=mesh['z'=8,'core'=2,'col'=16] {'z'}, dimensions={0} | all-to-all | bytes 458752 | tf_op jit(solution)/shard_map/all_to_all | solution.py:324
  21.1 2.4 %collective-permute-start = (bf16[8,7,16,128]{3,2,1,0:T(8,128)(2,1)S(1)}, bf16[8,7,16,128]{3,2,1,0:T(8,128)(2,1)S(1)}, u32[]{:S(2)}, u32[]{:S(2)}) collective-permute-start(bf16[8,7,16,128]{3,2,1,0:T(8,128)(2,1)S(1)} %all_to_all.20.near_ref), channel_id=1, source_target_pairs={{0,16},{16,0},{1,17},{17,1},{2,18},{18,2},{3,19},{19,3},{4,20},{20... | collective-permute-start | bytes 688136 | tf_op jit(solution)/shard_map/ppermute | solution.py:325
  23.5 1.1 %collective-permute-done.far_ref = bf16[8,7,16,128]{3,2,1,0:T(8,128)(2,1)S(1)} collective-permute-done((bf16[8,7,16,128]{3,2,1,0:T(8,128)(2,1)S(1)}, bf16[8,7,16,128]{3,2,1,0:T(8,128)(2,1)S(1)}, u32[]{:S(2)}, u32[]{:S(2)}) %collective-permute-start) | collective-permute-done | bytes 229408 | tf_op jit(solution)/shard_map/ppermute | solution.py:325
  24.6 6.0 %tiles.1 = f32[16,5,16,128]{3,2,1,0:T(8,128)S(1)} custom-call(s32[96]{0:T(128)} %rows_hbm.1, s32[96,128]{1,0:T(8,128)} %cols_hbm.1, bf16[8,7,16,128]{3,2,1,0:T(8,128)(2,1)S(1)} %all_to_all.20.near_ref, bf16[8,7,16,128]{3,2,1,0:T(8,128)(2,1)S(1)} %collective-permute-done.far_ref, bf16[96,128,128]{2,1,0:T(8,128)(2,1)} %value_hbm.1), custom_call_target="tpu_custom_call" | custom-call | tf_op jit(solution)/shard_map/tiles/pallas_call | solution.py:326
  30.6 18.7 %all_to_all.21.got_ref = f32[16,5,16,128]{3,2,1,0:T(8,128)S(1)} all-to-all(f32[16,5,16,128]{3,2,1,0:T(8,128)S(1)} %tiles.1), channel_id=1, replica_groups=mesh['z'=8,'core'=2,'col'=16] {'col'}, dimensions={0} | all-to-all | bytes 1310720 | tf_op jit(solution)/shard_map/all_to_all | solution.py:342
  49.2 0.0 copy-done
  49.2 0.0 copy-done.1
  49.2 0.0 copy-done.2
  49.2 1.3 %correct.1 = (f32[16,512]{1,0:T(8,128)S(1)}, f32[16,8,128]{2,1,0:T(8,128)S(1)}) custom-call(s32[1024]{0:T(1024)S(1)} %copy-done.1, f32[16,5,16,128]{3,2,1,0:T(8,128)S(1)} %all_to_all.21.got_ref, s32[4,128]{1,0:T(4,128)S(1)} %bitcast.2, bf16[1024,512]{1,0:T(8,128)(2,1)S(1)} %copy-done), custom_call_target="tpu_custom_call" | custom-call | tf_op jit(solution)/shard_map/correct/pallas_call | solution.py:343
  50.5 12.1 %all_to_all.22.got_ref = f32[16,8,128]{2,1,0:T(8,128)S(1)} all-to-all(f32[16,8,128]{2,1,0:T(8,128)S(1)} %get-tuple-element.4), channel_id=1, replica_groups=mesh['z'=8,'core'=2,'col'=16] {'z','core'}, dimensions={0} | all-to-all | bytes 131072 | tf_op jit(solution)/shard_map/all_to_all | solution.py:350
  62.6 9.3 %all_to_all.23.got_ref = f32[16,8,128]{2,1,0:T(8,128)S(1)} all-to-all(f32[16,8,128]{2,1,0:T(8,128)S(1)} %add_up.1), channel_id=1, replica_groups=mesh['z'=8,'core'=2,'col'=16] {'col'}, dimensions={0} | all-to-all | bytes 131072 | tf_op jit(solution)/shard_map/all_to_all | solution.py:352
  71.9 0.9 %finish.1 = (f32[16,512]{1,0:T(8,128)}, f32[16,16]{1,0:T(8,128)}) custom-call(f32[16,8,128]{2,1,0:T(8,128)S(1)} %all_to_all.23.got_ref, f32[16,512]{1,0:T(8,128)S(1)} %get-tuple-element.5.image_ref), custom_call_target="tpu_custom_call" | custom-call | tf_op jit(solution)/shard_map/finish/pallas_call | solution.py:353
  (1 shorter events, 0.0 us)
Async XLA Ops:
  2.4 46.8 %copy-start = (bf16[1024,512]{1,0:T(8,128)(2,1)S(1)}, bf16[1024,512]{1,0:T(8,128)(2,1)}, u32[]{:S(2)}) copy-start(bf16[1024,512]{1,0:T(8,128)(2,1)} %weight_ref.1) | copy-start | bytes 3145732
  2.4 46.8 %copy-start.1 = (s32[1024]{0:T(1024)S(1)}, s32[1024]{0:T(1024)}, u32[]{:S(2)}) copy-start(s32[1024]{0:T(1024)} %ids.1) | copy-start | bytes 12292
  2.4 46.8 %copy-start.2 = (s32[512]{0:T(512)S(1)}, s32[512]{0:T(512)}, u32[]{:S(2)}) copy-start(s32[512]{0:T(512)} %param.8) | copy-start | bytes 6148
  21.1 3.5 %collective-permute-start = (bf16[8,7,16,128]{3,2,1,0:T(8,128)(2,1)S(1)}, bf16[8,7,16,128]{3,2,1,0:T(8,128)(2,1)S(1)}, u32[]{:S(2)}, u32[]{:S(2)}) collective-permute-start(bf16[8,7,16,128]{3,2,1,0:T(8,128)(2,1)S(1)} %all_to_all.20.near_ref), channel_id=1, source_target_pairs={{0,16},{16,0},{1,17},{17,1},{2,18},{18,2},{3,19},{19,3},{4,20},{20... | collective-permute-start | bytes 688136 | tf_op jit(solution)/shard_map/ppermute | solution.py:325

commit v3 on v2

--- a/solution.py
+++ b/solution.py
@@ -37,9 +37,26 @@
 
 
 def prepare(
-    ids_hbm, x_hbm, degree_hbm, weight_hbm, out_ref, ids, x_ref, degree_ref, weight_ref, done
+    ids_hbm,
+    x_hbm,
+    degree_hbm,
+    weight_hbm,
+    cols_hbm,
+    out_ref,
+    cols_ref,
+    ids,
+    x_ref,
+    degree_ref,
+    weight_ref,
+    done,
 ):
-    pairs = ((weight_hbm, weight_ref), (x_hbm, x_ref), (degree_hbm, degree_ref), (ids_hbm, ids))
+    pairs = (
+        (weight_hbm, weight_ref),
+        (cols_hbm, cols_ref),
+        (x_hbm, x_ref),
+        (degree_hbm, degree_ref),
+        (ids_hbm, ids),
+    )
     copies = [pltpu.make_async_copy(a, b, done.at[n]) for n, (a, b) in enumerate(pairs)]
     for copy in copies:
         copy.start()
@@ -50,7 +67,7 @@
     own = ids.shape[0] // (2 * peers * lax.axis_size("col"))
     lane = lane_of(count)
     place = lane_of(count, width)
-    for copy in copies[1:]:
+    for copy in copies[2:]:
         copy.wait()
     x = x_ref[...]
     wide = x.astype(f32)
@@ -80,40 +97,110 @@
         odd = jnp.where(lane < 64, pltpu.roll(head, 64, 1), tail)
         out_ref[s, 4] = even.astype(bf16)
         out_ref[s, 5] = odd.astype(bf16)
+    copies[1].wait()
+
+
+def fill(table, got_ref):
+    count = got_ref.shape[2]
+    for z in range(got_ref.shape[0]):
+        for r in range(4):
+            at = pl.ds((z * 2 + r // 2) * count, count)
+            table[at, (r % 2) * LANES : (r % 2 + 1) * LANES] = got_ref[z, r]
+
+
+def pick_two(cols_ref, t, table, core, before):
+    hot, high, made = [], [], []
+    for e in range(2):
+        at = cols_ref[pl.ds(t + e, 1), :]
+        high.append(jnp.broadcast_to((at >> 8) - core * 2, (8, LANES)))
+        low = (at & 255).astype(jnp.int16)
+        place = lax.broadcasted_iota(jnp.int16, (2 * LANES, LANES), 0)
+        hot.append(jnp.where(place == low, jnp.ones((), bf16), jnp.zeros((), bf16)))
+    found = jnp.dot(table[...], jnp.concatenate(hot, 1), preferred_element_type=f32)
+    count = before[0].shape[0]
+    for e in range(2):
+        halves = [before[e][q * 8 : q * 8 + 8].astype(f32) for q in range(2)]
+        for h in range(table.shape[0] // count):
+            mask = high[e] == (h // 2) * 4 + h % 2
+            for q in range(2):
+                at = h * count + q * 8
+                part = found[at : at + 8, e * LANES : (e + 1) * LANES]
+                halves[q] = jnp.where(mask, part, halves[q])
+        made.append(jnp.concatenate(halves, 0).astype(bf16))
+    return made
+
+
+def pick_one(cols_ref, t, got_ref, core, before):
+    at = cols_ref[pl.ds(t, 1), :]
+    count = got_ref.shape[2]
+    low = jnp.broadcast_to(at & (LANES - 1), (count, LANES)).astype(jnp.int16)
+    high = jnp.broadcast_to((at >> 7) - core * 4, (count, LANES)).astype(jnp.int16)
+    dims = lax.GatherDimensionNumbers(
+        offset_dims=(),
+        collapsed_slice_dims=(1,),
+        start_index_map=(1,),
+        operand_batching_dims=(0,),
+        start_indices_batching_dims=(0,),
+    )
+    made = before
+    for z in range(got_ref.shape[0]):
+        for r in range(4):
+            moved = lax.gather(
+                got_ref[z, r],
+                low[:, :, None],
+                dims,
+                (1, 1),
+                mode=lax.GatherScatterMode.PROMISE_IN_BOUNDS,
+            )
+            made = jnp.where(high == jnp.int16(z * 8 + r), moved, made)
+    return made
+
+
+TWOS, ONES = 16, 16
+STEP = 2 * TWOS + ONES
+
+
+def pick(cols_ref, n, table, got_ref, core, before):
+    made = []
+    for u in range(0, 2 * TWOS, 2):
+        t = n * STEP + u
+        made += pick_two(cols_ref, t, table, core, (before(t), before(t + 1)))
+    for u in range(2 * TWOS, STEP):
+        t = n * STEP + u
+        made.append(pick_one(cols_ref, t, got_ref, core, before(t)))
+    return made
+
+
+def near_tiles(cols_ref, near_ref, value_hbm, value_ref, part_ref, table, done):
+    copy = pltpu.make_async_copy(value_hbm, value_ref, done.at[0])
+    copy.start()
+    core = lax.axis_index("core")
+    fill(table, near_ref)
+    zero = jnp.zeros(part_ref.shape[1:], bf16)
+
+    def some(n, carry):
+        made = pick(cols_ref, n, table, near_ref, core, lambda t: zero)
+        for u in range(STEP):
+            part_ref[n * STEP + u] = made[u]
+        return carry
+
+    lax.fori_loop(0, part_ref.shape[0] // STEP, some, 0)
+    copy.wait()
 
 
 def tiles(
-    rows_hbm,
-    cols_hbm,
-    near_ref,
-    far_ref,
-    value_hbm,
-    out_ref,
-    rows,
-    cols_ref,
-    value_ref,
-    table,
-    blocks,
-    picked,
-    done,
+    rows_hbm, cols_ref, near_ref, far_ref, part_ref, value_ref, out_ref, rows, table, picked, done
 ):
-    pairs = ((cols_hbm, cols_ref), (rows_hbm, rows), (value_hbm, value_ref))
-    copies = [pltpu.make_async_copy(a, b, done.at[n]) for n, (a, b) in enumerate(pairs)]
-    for copy in copies:
-        copy.start()
+    copy = pltpu.make_async_copy(rows_hbm, rows, done.at[0])
+    copy.start()
     peers, _, count, _ = out_ref.shape
-    tile_count = cols_ref.shape[0]
     core = lax.axis_index("core")
     lane = lane_of(count)
+    fill(table, far_ref)
     sums = jnp.zeros((count, LANES), f32)
     extra = jnp.zeros((count, LANES), f32)
-    for side, got_ref in ((core, near_ref), (1 - core, far_ref)):
+    for got_ref in (near_ref, far_ref):
         for z in range(got_ref.shape[0]):
-            for r in range(4):
-                block = got_ref[z, r]
-                at = pl.multiple_of((z * 4 + side * 2 + r // 2) * count, count)
-                table[pl.ds(at, count), (r % 2) * LANES : (r % 2 + 1) * LANES] = block
-                blocks[z * 8 + side * 4 + r] = block.astype(f32)
             sums += got_ref[z, 4 + core].astype(f32)
             extra += got_ref[z, 6].astype(f32)
     along = lane_sum(jnp.where((lane >= 64) & (lane < 67), extra, 0.0))
@@ -125,75 +212,37 @@
         block = jnp.where(lane == 64 + (4 * s + 4) % 64, along, base)
         out_ref[s, 4] = jnp.where(lane == 64 + (4 * s + 5) % 64, total, block)
 
-    def pick_two(t):
-        hot, high, made = [], [], []
-        for e in range(2):
-            at = cols_ref[pl.ds(t + e, 1), :]
-            high.append(jnp.broadcast_to(at >> 8, (8, LANES)))
-            low = (at & 255).astype(jnp.int16)
-            place = lax.broadcasted_iota(jnp.int16, (2 * LANES, LANES), 0)
-            hot.append(jnp.where(place == low, jnp.ones((), bf16), jnp.zeros((), bf16)))
-        found = jnp.dot(table[...], jnp.concatenate(hot, 1), preferred_element_type=f32)
-        for e in range(2):
-            halves = [jnp.zeros((8, LANES), f32)] * 2
-            for h in range(table.shape[0] // count):
-                mask = high[e] == h
-                for q in range(2):
-                    at = h * count + q * 8
-                    part = found[at : at + 8, e * LANES : (e + 1) * LANES]
-                    halves[q] = jnp.where(mask, part, halves[q])
-            made.append(jnp.concatenate(halves, 0).astype(bf16))
+    def choose(n):
+        return pick(cols_ref, n, table, far_ref, 1 - core, lambda t: part_ref[t])
+
+    def multiply(n):
+        made = []
+        for u in range(0, STEP, 2):
+            t = n * STEP + u
+            left = jnp.concatenate([picked[t], picked[t + 1]], 0)
+            right = jnp.concatenate([value_ref[t], value_ref[t + 1]], 0)
+            both = dot_t(left, right)
+            made += [both[:count, :LANES], both[count:, LANES:]]
         return made
 
-    def pick_one(t):
-        at = cols_ref[pl.ds(t, 1), :]
-        low = jnp.broadcast_to(at & (LANES - 1), (8, LANES))
-        high = jnp.broadcast_to(at >> 7, (8, LANES))
-        halves = [jnp.zeros((8, LANES), f32)] * 2
-        for h in range(blocks.shape[0]):
-            mask = high == h
-            for q in range(2):
-                part = jnp.take_along_axis(blocks[h, q * 8 : q * 8 + 8], low, axis=1)
-                halves[q] = jnp.where(mask, part, halves[q])
-        return jnp.concatenate(halves, 0).astype(bf16)
-
-    twos, ones = 8, 8
-    step = 2 * twos + ones
-
-    def pick(n):
-        made = []
-        for u in range(twos):
-            made += pick_two(n * step + 2 * u)
-        for u in range(ones):
-            made.append(pick_one(n * step + 2 * twos + u))
-        return made
-
-    def multiply(n):
-        return [dot_t(picked[n * step + u], value_ref[n * step + u]) for u in range(step)]
-
     def add(n, made):
-        for u in range(step):
-            at = rows[n * step + u]
+        for u in range(STEP):
+            at = rows[n * STEP + u]
             out_ref[at >> 2, at & 3] += made[u]
 
     def keep(n, made):
-        for u in range(step):
-            picked[n * step + u] = made[u]
-
-    copies[0].wait()
-    keep(0, pick(0))
-    copies[1].wait()
-    copies[2].wait()
-
-    def both(n, carry):
+        for u in range(STEP):
+            picked[n * STEP + u] = made[u]
+
+    keep(0, choose(0))
+    copy.wait()
+    steps = part_ref.shape[0] // STEP
+    for n in range(1, steps):
         products = multiply(n - 1)
-        made = pick(n)
+        made = choose(n)
         add(n - 1, products)
         keep(n, made)
-        return carry
-
-    lax.fori_loop(1, tile_count // step, both, 0)
-    add(tile_count // step - 1, multiply(tile_count // step - 1))
+    add(steps - 1, multiply(steps - 1))
 
 
 def correct(ids, got_ref, degree_ref, weight_ref, image_ref, out_ref):
@@ -307,10 +356,10 @@
             name=name,
         )
 
-    sent = call(
+    sent, cols = call(
         prepare,
-        shape((z_n, 7, count, LANES), bf16),
-        [hbm] * 4,
+        (shape((z_n, 7, count, LANES), bf16), pltpu.VMEM(tile_cols.shape, i32)),
+        [hbm] * 5,
         8,
         "prepare",
         [
@@ -318,27 +367,33 @@
             pltpu.VMEM(vectors.shape, bf16),
             pltpu.VMEM(degree_rows.shape, i32),
             pltpu.VMEM(hub_weight.shape, bf16),
-            pltpu.SemaphoreType.DMA((4,)),
+            pltpu.SemaphoreType.DMA((5,)),
         ],
-    )(stay(hub_ids), stay(vectors), stay(degree_rows), stay(hub_weight))
+    )(stay(hub_ids), stay(vectors), stay(degree_rows), stay(hub_weight), stay(tile_cols))
     near = lax.all_to_all(sent, "z", 0, 0)
     far = lax.ppermute(near, "core", [(0, 1), (1, 0)])
+    table = pltpu.VMEM((rows_n * count, 2 * LANES), bf16)
+    values, part = call(
+        near_tiles,
+        (pltpu.VMEM(tile_values.shape, bf16), pltpu.VMEM((tile_count, count, LANES), bf16)),
+        [vmem, vmem, hbm],
+        16,
+        "near_tiles",
+        [table, pltpu.SemaphoreType.DMA((1,))],
+    )(cols, near, stay(tile_values))
     sent = call(
         tiles,
         shape((cols_n, 5, count, LANES), f32),
-        [hbm, hbm, vmem, vmem, hbm],
-        24,
+        [hbm, vmem, vmem, vmem, vmem, vmem],
+        16,
         "tiles",
         [
             pltpu.SMEM(tile_rows.shape, i32),
-            pltpu.VMEM(tile_cols.shape, i32),
-            pltpu.VMEM(tile_values.shape, bf16),
-            pltpu.VMEM((2 * rows_n * count, 2 * LANES), bf16),
-            pltpu.VMEM((4 * rows_n, count, LANES), f32),
+            table,
             pltpu.VMEM((tile_count, count, LANES), bf16),
-            pltpu.SemaphoreType.DMA((3,)),
+            pltpu.SemaphoreType.DMA((1,)),
         ],
-    )(stay(tile_rows), stay(tile_cols), near, far, stay(tile_values))
+    )(stay(tile_rows), cols, near, far, part, values)
     got = lax.all_to_all(sent, "col", 0, 0)
     image, sent = call(
         correct,

time: 73.2 us -> 70.5 us (0.963)
  Pallas kernels: 9.91 us -> 8.48 us
  waiting for transfers between devices: 1.12 us -> 0.01 us
    pallas_call x2 -> x3, Pallas kernels: 7.68 us -> 6.25 us  [the longest x1 2.61 us: on_device(): call(tiles, shape((cols_n, 5, count, LANES), f32), [hbm, vmem, vmem, vmem...]
    ppermute x1, waiting for transfers between devices: 1.12 us -> 0.01 us  [on_device(): far = lax.ppermute(near, 'core', [(0, 1), (1, 0)])]
  transfers between devices with their start and end apart: 1 -> 1, of which waited for: 1 -> 0; matrix products, arithmetic and copies ran while one was open for 0% -> 0% of each run, Pallas kernels for 0% -> 3%
where the time goes in v3:
time: 70.5 us; the launch traced here: 70.2 us
  blocking collectives  58.6 us (83%)
  Pallas kernels  8.48 us (12%)
  starting transfers between devices  2.38 us (3%)
    all_to_all x2, blocking collectives, on_device(): got = lax.all_to_all(sent, 'col', 0, 0)  28.7 us
    all_to_all x1, blocking collectives, on_device(): near = lax.all_to_all(sent, 'z', 0, 0)  18.6 us
    all_to_all x1, blocking collectives, on_device(): got = lax.all_to_all(sent, ('z', 'core'), 0, 0)  11.4 us
    pallas_call x1, Pallas kernels, on_device(): call(tiles, shape((cols_n, 5, count, LANES), f32), [hbm, vmem, vmem, vmem...  2.61 us
    ppermute x1, starting transfers between devices, on_device(): far = lax.ppermute(near, 'core', [(0, 1), (1, 0)])  2.38 us
    pallas_call x1, Pallas kernels, on_device(): call(near_tiles, (pltpu.VMEM(tile_values.shape, bf16), pltpu.VMEM((tile_c...  1.9 us
    pallas_call x1, Pallas kernels, on_device(): call(prepare, (shape((z_n, 7, count, LANES), bf16), pltpu.VMEM(tile_cols....  1.74 us
  transfers between devices with their start and end apart: 1, of which 0 were waited for; matrix products, arithmetic and copies ran while one was open for 0% of the time, Pallas kernels for 3%

profile of v3, /device:TPU:1, one launch (start us, length us, event | category | flops | bytes accessed | tf_op | source)
XLA Modules:
  0.0 70.2 jit_solution(16823299718064641901)
XLA Ops:
  0.6 1.7 %prepare.1 = (bf16[8,7,16,128]{3,2,1,0:T(8,128)(2,1)S(1)}, s32[96,128]{1,0:T(8,128)S(1)}) custom-call(s32[1024]{0:T(1024)} %ids.1, bf16[16,512]{1,0:T(8,128)(2,1)} %x_hbm.1, s32[4,128]{1,0:T(4,128)} %bitcast.1, bf16[1024,512]{1,0:T(8,128)(2,1)} %weight_ref.1, s32[96,128]{1,0:T(8,128)} %cols_hbm.1), custom_call_target="tpu_custom_call" | custom-call | tf_op jit(solution)/shard_map/prepare/pallas_call | solution.py:359
  2.4 18.6 %all_to_all.20.near_ref = bf16[8,7,16,128]{3,2,1,0:T(8,128)(2,1)S(1)} all-to-all(bf16[8,7,16,128]{3,2,1,0:T(8,128)(2,1)S(1)} %get-tuple-element.9), channel_id=1, replica_groups=mesh['z'=8,'core'=2,'col'=16] {'z'}, dimensions={0} | all-to-all | bytes 458752 | tf_op jit(solution)/shard_map/all_to_all | solution.py:373
  20.9 2.4 %collective-permute-start = (bf16[8,7,16,128]{3,2,1,0:T(8,128)(2,1)S(1)}, bf16[8,7,16,128]{3,2,1,0:T(8,128)(2,1)S(1)}, u32[]{:S(2)}, u32[]{:S(2)}) collective-permute-start(bf16[8,7,16,128]{3,2,1,0:T(8,128)(2,1)S(1)} %all_to_all.20.near_ref), channel_id=1, source_target_pairs={{0,16},{16,0},{1,17},{17,1},{2,18},{18,2},{3,19},{19,3},{4,20},{20... | collective-permute-start | bytes 688136 | tf_op jit(solution)/shard_map/ppermute | solution.py:374
  23.3 1.9 %near_tiles.1 = (bf16[96,128,128]{2,1,0:T(8,128)(2,1)S(1)}, bf16[96,16,128]{2,1,0:T(8,128)(2,1)S(1)}) custom-call(s32[96,128]{1,0:T(8,128)S(1)} %get-tuple-element.8.cols_ref, bf16[8,7,16,128]{3,2,1,0:T(8,128)(2,1)S(1)} %all_to_all.20.near_ref, bf16[96,128,128]{2,1,0:T(8,128)(2,1)} %value_hbm.1), custom_call_target="tpu_custom_call" | custom-call | tf_op jit(solution)/shard_map/near_tiles/pallas_call | solution.py:376
  25.2 0.0 copy-start
  25.2 0.0 copy-start.1
  25.3 0.0 copy-start.2
  25.3 0.0 collective-permute-done.far_ref
  25.3 2.6 %tiles.1 = f32[16,5,16,128]{3,2,1,0:T(8,128)S(1)} custom-call(s32[96]{0:T(128)} %rows_hbm.1, s32[96,128]{1,0:T(8,128)S(1)} %get-tuple-element.8.cols_ref, bf16[8,7,16,128]{3,2,1,0:T(8,128)(2,1)S(1)} %all_to_all.20.near_ref, bf16[8,7,16,128]{3,2,1,0:T(8,128)(2,1)S(1)} %collective-permute-done.far_ref, bf16[96,16,128]{2,1,0:T(8,128)(2,1)S(1)} %get-tuple-element.10.part_ref, ...), custom_call_target="tpu_custom_call" | custom-call | tf_op jit(solution)/shard_map/tiles/pallas_call | solution.py:384
  27.9 19.3 %all_to_all.21.got_ref = f32[16,5,16,128]{3,2,1,0:T(8,128)S(1)} all-to-all(f32[16,5,16,128]{3,2,1,0:T(8,128)S(1)} %tiles.1), channel_id=1, replica_groups=mesh['z'=8,'core'=2,'col'=16] {'col'}, dimensions={0} | all-to-all | bytes 1310720 | tf_op jit(solution)/shard_map/all_to_all | solution.py:397
  47.2 0.0 copy-done
  47.2 0.0 copy-done.1
  47.2 0.0 copy-done.2
  47.2 1.3 %correct.1 = (f32[16,512]{1,0:T(8,128)S(1)}, f32[16,8,128]{2,1,0:T(8,128)S(1)}) custom-call(s32[1024]{0:T(1024)S(1)} %copy-done.1, f32[16,5,16,128]{3,2,1,0:T(8,128)S(1)} %all_to_all.21.got_ref, s32[4,128]{1,0:T(4,128)S(1)} %bitcast.2, bf16[1024,512]{1,0:T(8,128)(2,1)S(1)} %copy-done), custom_call_target="tpu_custom_call" | custom-call | tf_op jit(solution)/shard_map/correct/pallas_call | solution.py:398
  48.5 11.4 %all_to_all.22.got_ref = f32[16,8,128]{2,1,0:T(8,128)S(1)} all-to-all(f32[16,8,128]{2,1,0:T(8,128)S(1)} %get-tuple-element.12), channel_id=1, replica_groups=mesh['z'=8,'core'=2,'col'=16] {'z','core'}, dimensions={0} | all-to-all | bytes 131072 | tf_op jit(solution)/shard_map/all_to_all | solution.py:405
  60.0 9.3 %all_to_all.23.got_ref = f32[16,8,128]{2,1,0:T(8,128)S(1)} all-to-all(f32[16,8,128]{2,1,0:T(8,128)S(1)} %add_up.1), channel_id=1, replica_groups=mesh['z'=8,'core'=2,'col'=16] {'col'}, dimensions={0} | all-to-all | bytes 131072 | tf_op jit(solution)/shard_map/all_to_all | solution.py:407
  69.3 0.9 %finish.1 = (f32[16,512]{1,0:T(8,128)}, f32[16,16]{1,0:T(8,128)}) custom-call(f32[16,8,128]{2,1,0:T(8,128)S(1)} %all_to_all.23.got_ref, f32[16,512]{1,0:T(8,128)S(1)} %get-tuple-element.13.image_ref), custom_call_target="tpu_custom_call" | custom-call | tf_op jit(solution)/shard_map/finish/pallas_call | solution.py:408
  (1 shorter events, 0.0 us)
Async XLA Ops:
  20.9 4.3 %collective-permute-start = (bf16[8,7,16,128]{3,2,1,0:T(8,128)(2,1)S(1)}, bf16[8,7,16,128]{3,2,1,0:T(8,128)(2,1)S(1)}, u32[]{:S(2)}, u32[]{:S(2)}) collective-permute-start(bf16[8,7,16,128]{3,2,1,0:T(8,128)(2,1)S(1)} %all_to_all.20.near_ref), channel_id=1, source_target_pairs={{0,16},{16,0},{1,17},{17,1},{2,18},{18,2},{3,19},{19,3},{4,20},{20... | collective-permute-start | bytes 688136 | tf_op jit(solution)/shard_map/ppermute | solution.py:374
  25.2 22.0 %copy-start = (bf16[1024,512]{1,0:T(8,128)(2,1)S(1)}, bf16[1024,512]{1,0:T(8,128)(2,1)}, u32[]{:S(2)}) copy-start(bf16[1024,512]{1,0:T(8,128)(2,1)} %weight_ref.1) | copy-start | bytes 3145732
  25.2 22.0 %copy-start.1 = (s32[1024]{0:T(1024)S(1)}, s32[1024]{0:T(1024)}, u32[]{:S(2)}) copy-start(s32[1024]{0:T(1024)} %ids.1) | copy-start | bytes 12292
  25.3 22.0 %copy-start.2 = (s32[512]{0:T(512)S(1)}, s32[512]{0:T(512)}, u32[]{:S(2)}) copy-start(s32[512]{0:T(512)} %param.8) | copy-start | bytes 6148

commit v4 on v3

--- a/solution.py
+++ b/solution.py
@@ -44,6 +44,7 @@
     cols_hbm,
     out_ref,
     cols_ref,
+    mark_ref,
     ids,
     x_ref,
     degree_ref,
@@ -52,10 +53,10 @@
 ):
     pairs = (
         (weight_hbm, weight_ref),
-        (cols_hbm, cols_ref),
         (x_hbm, x_ref),
         (degree_hbm, degree_ref),
         (ids_hbm, ids),
+        (cols_hbm, cols_ref),
     )
     copies = [pltpu.make_async_copy(a, b, done.at[n]) for n, (a, b) in enumerate(pairs)]
     for copy in copies:
@@ -66,8 +67,8 @@
     width = x_ref.shape[1]
     own = ids.shape[0] // (2 * peers * lax.axis_size("col"))
     lane = lane_of(count)
-    place = lane_of(count, width)
-    for copy in copies[2:]:
+    place = lane_of(1, width)
+    for copy in copies[1:4]:
         copy.wait()
     x = x_ref[...]
     wide = x.astype(f32)
@@ -79,9 +80,9 @@
     total = lane_sum(jnp.sum(degrees, axis=0, keepdims=True))
     extra = jnp.zeros((count, LANES), f32)
     for k in range(own):
-        offset = ids[piece * own + k] - piece * width
-        value = lane_sum(jnp.where(place == offset, wide, 0.0))
-        extra = jnp.where(lane == row * own + k, value, extra)
+        mark = jnp.where(place == ids[piece * own + k] - piece * width, 1.0, 0.0)
+        mark_ref[k : k + 1, :] = mark
+        extra = jnp.where(lane == row * own + k, lane_sum(wide * mark), extra)
     for at, value in enumerate(pieces(along, 3) + pieces(total, 2)):
         extra = jnp.where(lane == 64 + at, value, extra)
     extra = extra.astype(bf16)
@@ -97,7 +98,7 @@
         odd = jnp.where(lane < 64, pltpu.roll(head, 64, 1), tail)
         out_ref[s, 4] = even.astype(bf16)
         out_ref[s, 5] = odd.astype(bf16)
-    copies[1].wait()
+    copies[-1].wait()
 
 
 def fill(table, got_ref):
@@ -156,17 +157,13 @@
     return made
 
 
-TWOS, ONES = 16, 16
-STEP = 2 * TWOS + ONES
-
-
-def pick(cols_ref, n, table, got_ref, core, before):
+def pick(cols_ref, first, step, twos, table, got_ref, core, before):
     made = []
-    for u in range(0, 2 * TWOS, 2):
-        t = n * STEP + u
+    for t in range(0, 2 * twos, 2):
+        t = first + t
         made += pick_two(cols_ref, t, table, core, (before(t), before(t + 1)))
-    for u in range(2 * TWOS, STEP):
-        t = n * STEP + u
+    for t in range(2 * twos, step):
+        t = first + t
         made.append(pick_one(cols_ref, t, got_ref, core, before(t)))
     return made
 
@@ -177,14 +174,15 @@
     core = lax.axis_index("core")
     fill(table, near_ref)
     zero = jnp.zeros(part_ref.shape[1:], bf16)
+    step = 48
 
     def some(n, carry):
-        made = pick(cols_ref, n, table, near_ref, core, lambda t: zero)
-        for u in range(STEP):
-            part_ref[n * STEP + u] = made[u]
+        made = pick(cols_ref, n * step, step, 16, table, near_ref, core, lambda t: zero)
+        for u in range(step):
+            part_ref[n * step + u] = made[u]
         return carry
 
-    lax.fori_loop(0, part_ref.shape[0] // STEP, some, 0)
+    lax.fori_loop(0, part_ref.shape[0] // step, some, 0)
     copy.wait()
 
 
@@ -205,6 +203,8 @@
             extra += got_ref[z, 6].astype(f32)
     along = lane_sum(jnp.where((lane >= 64) & (lane < 67), extra, 0.0))
     total = lane_sum(jnp.where((lane >= 67) & (lane < 69), extra, 0.0))
+    origin = 8 * ((((lane & 31) >> 2) - lax.axis_index("col")) & 7) + 4 * (lane >> 5) + (lane & 3)
+    extra = jnp.take_along_axis(extra, origin & (LANES - 1), axis=1)
     base = jnp.where(lane < 64, extra, sums + pltpu.roll(sums, 64, 1))
     for s in range(peers):
         for r in range(4):
@@ -212,13 +212,15 @@
         block = jnp.where(lane == 64 + (4 * s + 4) % 64, along, base)
         out_ref[s, 4] = jnp.where(lane == 64 + (4 * s + 5) % 64, total, block)
 
+    step, twos = 48, 16
+
     def choose(n):
-        return pick(cols_ref, n, table, far_ref, 1 - core, lambda t: part_ref[t])
+        return pick(cols_ref, n * step, step, twos, table, far_ref, 1 - core, lambda t: part_ref[t])
 
     def multiply(n):
         made = []
-        for u in range(0, STEP, 2):
-            t = n * STEP + u
+        for u in range(0, step, 2):
+            t = n * step + u
             left = jnp.concatenate([picked[t], picked[t + 1]], 0)
             right = jnp.concatenate([value_ref[t], value_ref[t + 1]], 0)
             both = dot_t(left, right)
@@ -226,17 +228,17 @@
         return made
 
     def add(n, made):
-        for u in range(STEP):
-            at = rows[n * STEP + u]
+        for u in range(step):
+            at = rows[n * step + u]
             out_ref[at >> 2, at & 3] += made[u]
 
     def keep(n, made):
-        for u in range(STEP):
-            picked[n * STEP + u] = made[u]
+        for u in range(step):
+            picked[n * step + u] = made[u]
 
     keep(0, choose(0))
     copy.wait()
-    steps = part_ref.shape[0] // STEP
+    steps = part_ref.shape[0] // step
     for n in range(1, steps):
         products = multiply(n - 1)
         made = choose(n)
@@ -245,16 +247,23 @@
     add(steps - 1, multiply(steps - 1))
 
 
-def correct(ids, got_ref, degree_ref, weight_ref, image_ref, out_ref):
+def correct(mark_ref, got_ref, degree_ref, weight_ref, image_ref, out_ref):
     j = lax.axis_index("col")
-    row = lax.axis_index("z") * 2 + lax.axis_index("core")
-    piece = row * lax.axis_size("col") + j
     peers, _, count, _ = got_ref.shape
-    width = degree_ref.shape[0] * LANES
-    own = ids.shape[0] // (peers * out_ref.shape[0])
+    own, width = mark_ref.shape
     lane = lane_of(count)
-    half = lane_of(8)
-    source = (half & 63) >> 2
+    group = (lane & 31) >> 2
+    values = []
+    for m in range(weight_ref.shape[0] // LANES):
+        sides = []
+        for first in (0, peers // 2):
+            found = got_ref[first, 4]
+            for s in range(first + 1, first + peers // 2):
+                found = jnp.where(group == (m + s) % 8, got_ref[s, 4], found)
+            at = 32 * (lane >> 6) + 4 * ((m + ((lane >> 2) & 7)) & 7) + (lane & 3)
+            sides.append(jnp.take_along_axis(found, at, axis=1))
+        values.append(jnp.where((lane & 32) == 0, sides[0], sides[1]).astype(bf16))
+    hub = jnp.dot(jnp.concatenate(values, 1), weight_ref[...], preferred_element_type=f32)
     blocks = []
     for r in range(5):
         total = got_ref[0, r]
@@ -262,29 +271,19 @@
             total += got_ref[s, r]
         blocks.append(total)
     extra = blocks[4]
-    pick = lambda at: lane_sum(jnp.where(lane == at, extra, 0.0))
-    ratio = pick(64 + ((4 * j + 4) & 63)) / pick(64 + ((4 * j + 5) & 63))
-    values = []
-    for m in range(ids.shape[0] // LANES):
-        at = 8 * m + 4 * (half >> 6) + (half & 3)
-        parts = []
-        for q in range(2):
-            found = jnp.zeros((8, LANES), f32)
-            for s in range(peers):
-                moved = jnp.take_along_axis(got_ref[s, 4, 8 * q : 8 * q + 8], at, axis=1)
-                found = jnp.where(source == s, moved, found)
-            parts.append(found)
-        values.append(jnp.concatenate(parts, 0).astype(bf16))
-    hub = jnp.dot(jnp.concatenate(values, 1), weight_ref[...], preferred_element_type=f32)
+    at_lane = lambda at: lane_sum(jnp.where(lane == at, extra, 0.0))
+    ratio = at_lane(64 + ((4 * j + 4) & 63)) / at_lane(64 + ((4 * j + 5) & 63))
     degrees = degree_ref[...].astype(f32)
-    hub_at = [ids[piece * own + k] - piece * width for k in range(own)]
-    hub_sum = [pick(64 + 4 * j + k) for k in range(own)]
+    hub_sum = [at_lane(64 + 4 * j + k) for k in range(own)]
+    parts = []
     for r in range(width // LANES):
-        block = blocks[r] + hub[:, r * LANES : (r + 1) * LANES]
+        columns = slice(r * LANES, (r + 1) * LANES)
+        block = blocks[r] - ratio * degrees[r : r + 1]
         for k in range(own):
-            block += jnp.where(lane + r * LANES == hub_at[k], hub_sum[k], 0.0)
-        image_ref[:, r * LANES : (r + 1) * LANES] = block - ratio * degrees[r : r + 1]
-    image = image_ref[...]
+            block += hub_sum[k] * mark_ref[k : k + 1, columns]
+        parts.append(block + hub[:, columns])
+        image_ref[:, columns] = parts[r]
+    image = jnp.concatenate(parts, 1)
     gram = dot_t(image, image, lax.Precision.HIGHEST)
     packed = jnp.concatenate([gram[0:8], gram[8:16], jnp.zeros((8, LANES - 32), f32)], 1)
     for s in range(out_ref.shape[0]):
@@ -336,7 +335,7 @@
     z_n, cols_n = lax.axis_size("z"), lax.axis_size("col")
     rows_n = 2 * z_n
     tile_count = tile_values.shape[0]
-    smem = pl.BlockSpec(memory_space=pltpu.SMEM)
+    own = hub_ids.shape[0] // (rows_n * cols_n)
     vmem = pl.BlockSpec(memory_space=pltpu.VMEM)
     hbm = pl.BlockSpec(memory_space=pltpu.HBM)
     shape = jax.ShapeDtypeStruct
@@ -356,9 +355,13 @@
             name=name,
         )
 
-    sent, cols = call(
+    sent, cols, marks = call(
         prepare,
-        (shape((z_n, 7, count, LANES), bf16), pltpu.VMEM(tile_cols.shape, i32)),
+        (
+            shape((z_n, 7, count, LANES), bf16),
+            pltpu.VMEM(tile_cols.shape, i32),
+            shape((own, width), f32),
+        ),
         [hbm] * 5,
         8,
         "prepare",
@@ -398,10 +401,10 @@
     image, sent = call(
         correct,
         (shape((count, width), f32), shape((rows_n, 8, LANES), f32)),
-        [smem, vmem, vmem, vmem],
+        [vmem, vmem, vmem, vmem],
         8,
         "correct",
-    )(hub_ids, got, degree_rows, hub_weight)
+    )(marks, got, degree_rows, hub_weight)
     got = lax.all_to_all(sent, ("z", "core"), 0, 0)
     sent = call(add_up, shape((cols_n, 8, LANES), f32), [vmem], 4, "add_up")(got)
     got = lax.all_to_all(sent, "col", 0, 0)

time: 70.5 us -> 69.7 us (0.989)
  Pallas kernels: 8.48 us -> 7.67 us
    pallas_call x1, Pallas kernels: 1.27 us -> 0.48 us  [on_device(): call(correct, (shape((count, width), f32), shape((rows_n, 8, LANES), f32)...]
where the time goes in v4:
time: 69.7 us; the launch traced here: 69.4 us
  blocking collectives  58.6 us (84%)
  Pallas kernels  7.67 us (11%)
  starting transfers between devices  2.38 us (3%)
    all_to_all x2, blocking collectives, on_device(): got = lax.all_to_all(sent, 'col', 0, 0)  28.6 us
    all_to_all x1, blocking collectives, on_device(): near = lax.all_to_all(sent, 'z', 0, 0)  18.6 us
    all_to_all x1, blocking collectives, on_device(): got = lax.all_to_all(sent, ('z', 'core'), 0, 0)  11.4 us
    pallas_call x1, Pallas kernels, on_device(): call(tiles, shape((cols_n, 5, count, LANES), f32), [hbm, vmem, vmem, vmem...  2.59 us
    ppermute x1, starting transfers between devices, on_device(): far = lax.ppermute(near, 'core', [(0, 1), (1, 0)])  2.38 us
    pallas_call x1, Pallas kernels, on_device(): call(near_tiles, (pltpu.VMEM(tile_values.shape, bf16), pltpu.VMEM((tile_c...  1.9 us
    pallas_call x1, Pallas kernels, on_device(): call(prepare, (shape((z_n, 7, count, LANES), bf16), pltpu.VMEM(tile_cols....  1.74 us
  transfers between devices with their start and end apart: 1, of which 0 were waited for; matrix products, arithmetic and copies ran while one was open for 0% of the time, Pallas kernels for 3%

profile of v4, /device:TPU:1, one launch (start us, length us, event | category | flops | bytes accessed | tf_op | source)
XLA Modules:
  0.0 69.4 jit_solution(13600185336057680540)
XLA Ops:
  0.6 1.7 %prepare.1 = (bf16[8,7,16,128]{3,2,1,0:T(8,128)(2,1)S(1)}, s32[96,128]{1,0:T(8,128)S(1)}, f32[4,512]{1,0:T(4,128)S(1)}) custom-call(s32[1024]{0:T(1024)} %ids_hbm.1, bf16[16,512]{1,0:T(8,128)(2,1)} %x_hbm.1, s32[4,128]{1,0:T(4,128)} %bitcast.1, bf16[1024,512]{1,0:T(8,128)(2,1)} %weight_ref.1, s32[96,128]{1,0:T(8,128)} %cols_hbm.1), custom_call_target="tpu_custom_call" | custom-call | tf_op jit(solution)/shard_map/prepare/pallas_call | solution.py:358
  2.4 18.6 %all_to_all.20.near_ref = bf16[8,7,16,128]{3,2,1,0:T(8,128)(2,1)S(1)} all-to-all(bf16[8,7,16,128]{3,2,1,0:T(8,128)(2,1)S(1)} %get-tuple-element.11), channel_id=1, replica_groups=mesh['z'=8,'core'=2,'col'=16] {'z'}, dimensions={0} | all-to-all | bytes 458752 | tf_op jit(solution)/shard_map/all_to_all | solution.py:376
  20.9 2.4 %collective-permute-start = (bf16[8,7,16,128]{3,2,1,0:T(8,128)(2,1)S(1)}, bf16[8,7,16,128]{3,2,1,0:T(8,128)(2,1)S(1)}, u32[]{:S(2)}, u32[]{:S(2)}) collective-permute-start(bf16[8,7,16,128]{3,2,1,0:T(8,128)(2,1)S(1)} %all_to_all.20.near_ref), channel_id=1, source_target_pairs={{0,16},{16,0},{1,17},{17,1},{2,18},{18,2},{3,19},{19,3},{4,20},{20... | collective-permute-start | bytes 688136 | tf_op jit(solution)/shard_map/ppermute | solution.py:377
  23.3 1.9 %near_tiles.1 = (bf16[96,128,128]{2,1,0:T(8,128)(2,1)S(1)}, bf16[96,16,128]{2,1,0:T(8,128)(2,1)S(1)}) custom-call(s32[96,128]{1,0:T(8,128)S(1)} %get-tuple-element.10.cols_ref, bf16[8,7,16,128]{3,2,1,0:T(8,128)(2,1)S(1)} %all_to_all.20.near_ref, bf16[96,128,128]{2,1,0:T(8,128)(2,1)} %value_hbm.1), custom_call_target="tpu_custom_call" | custom-call | tf_op jit(solution)/shard_map/near_tiles/pallas_call | solution.py:379
  25.2 0.0 copy-start
  25.2 0.0 copy-start.1
  25.3 0.0 collective-permute-done.far_ref
  25.3 2.6 %tiles.1 = f32[16,5,16,128]{3,2,1,0:T(8,128)S(1)} custom-call(s32[96]{0:T(128)} %rows_hbm.1, s32[96,128]{1,0:T(8,128)S(1)} %get-tuple-element.10.cols_ref, bf16[8,7,16,128]{3,2,1,0:T(8,128)(2,1)S(1)} %all_to_all.20.near_ref, bf16[8,7,16,128]{3,2,1,0:T(8,128)(2,1)S(1)} %collective-permute-done.far_ref, bf16[96,16,128]{2,1,0:T(8,128)(2,1)S(1)} %get-tuple-element.12.part_ref, ...), custom_call_target="tpu_custom_call" | custom-call | tf_op jit(solution)/shard_map/tiles/pallas_call | solution.py:387
  27.9 19.3 %all_to_all.21.got_ref = f32[16,5,16,128]{3,2,1,0:T(8,128)S(1)} all-to-all(f32[16,5,16,128]{3,2,1,0:T(8,128)S(1)} %tiles.1), channel_id=1, replica_groups=mesh['z'=8,'core'=2,'col'=16] {'col'}, dimensions={0} | all-to-all | bytes 1310720 | tf_op jit(solution)/shard_map/all_to_all | solution.py:400
  47.2 0.0 copy-done
  47.2 0.0 copy-done.1
  47.2 0.5 correct.1
  47.7 11.4 %all_to_all.22.got_ref = f32[16,8,128]{2,1,0:T(8,128)S(1)} all-to-all(f32[16,8,128]{2,1,0:T(8,128)S(1)} %get-tuple-element.14), channel_id=1, replica_groups=mesh['z'=8,'core'=2,'col'=16] {'z','core'}, dimensions={0} | all-to-all | bytes 131072 | tf_op jit(solution)/shard_map/all_to_all | solution.py:408
  59.1 9.3 %all_to_all.23.got_ref = f32[16,8,128]{2,1,0:T(8,128)S(1)} all-to-all(f32[16,8,128]{2,1,0:T(8,128)S(1)} %add_up.1), channel_id=1, replica_groups=mesh['z'=8,'core'=2,'col'=16] {'col'}, dimensions={0} | all-to-all | bytes 131072 | tf_op jit(solution)/shard_map/all_to_all | solution.py:410
  68.5 0.9 %finish.1 = (f32[16,512]{1,0:T(8,128)}, f32[16,16]{1,0:T(8,128)}) custom-call(f32[16,8,128]{2,1,0:T(8,128)S(1)} %all_to_all.23.got_ref, f32[16,512]{1,0:T(8,128)S(1)} %get-tuple-element.15.image_ref), custom_call_target="tpu_custom_call" | custom-call | tf_op jit(solution)/shard_map/finish/pallas_call | solution.py:411
  (1 shorter events, 0.0 us)
Async XLA Ops:
  20.9 4.3 %collective-permute-start = (bf16[8,7,16,128]{3,2,1,0:T(8,128)(2,1)S(1)}, bf16[8,7,16,128]{3,2,1,0:T(8,128)(2,1)S(1)}, u32[]{:S(2)}, u32[]{:S(2)}) collective-permute-start(bf16[8,7,16,128]{3,2,1,0:T(8,128)(2,1)S(1)} %all_to_all.20.near_ref), channel_id=1, source_target_pairs={{0,16},{16,0},{1,17},{17,1},{2,18},{18,2},{3,19},{19,3},{4,20},{20... | collective-permute-start | bytes 688136 | tf_op jit(solution)/shard_map/ppermute | solution.py:377
  25.2 22.0 %copy-start = (bf16[1024,512]{1,0:T(8,128)(2,1)S(1)}, bf16[1024,512]{1,0:T(8,128)(2,1)}, u32[]{:S(2)}) copy-start(bf16[1024,512]{1,0:T(8,128)(2,1)} %weight_ref.1) | copy-start | bytes 3145732
  25.2 22.0 %copy-start.1 = (s32[512]{0:T(512)S(1)}, s32[512]{0:T(512)}, u32[]{:S(2)}) copy-start(s32[512]{0:T(512)} %param.8) | copy-start | bytes 6148

commit v5 on v4

--- a/solution.py
+++ b/solution.py
@@ -34,6 +34,22 @@
         found.append(head)
         a = a - head
     return found
+
+
+UNIT = 8300000.0
+BIAS = 32768
+
+
+def exponent(top):
+    return jnp.ceil(jnp.log2(jnp.maximum(top, 1e-30)))
+
+
+def code(values, power, unit=UNIT):
+    return jnp.floor(values * (unit * jnp.exp2(-power)) + 0.5).astype(i32)
+
+
+def lane_max(a):
+    return jnp.max(jnp.abs(a), axis=1, keepdims=True)
 
 
 def prepare(
@@ -45,10 +61,10 @@
     out_ref,
     cols_ref,
     mark_ref,
+    degree_ref,
+    weight_ref,
     ids,
     x_ref,
-    degree_ref,
-    weight_ref,
     done,
 ):
     pairs = (
@@ -157,15 +173,18 @@
     return made
 
 
-def pick(cols_ref, first, step, twos, table, got_ref, core, before):
-    made = []
-    for t in range(0, 2 * twos, 2):
-        t = first + t
-        made += pick_two(cols_ref, t, table, core, (before(t), before(t + 1)))
-    for t in range(2 * twos, step):
-        t = first + t
-        made.append(pick_one(cols_ref, t, got_ref, core, before(t)))
-    return made
+def pick(cols_ref, first, step, twos, table, got_ref, core, before, beside=lambda: None):
+    pairs, singles = [], []
+    for n in range(twos):
+        t = first + 2 * n
+        beside()
+        pairs += pick_two(cols_ref, t, table, core, (before(t), before(t + 1)))
+        while len(singles) * twos < (n + 1) * (step - 2 * twos):
+            t = first + 2 * twos + len(singles)
+            if len(singles) % 2 == 0:
+                beside()
+            singles.append(pick_one(cols_ref, t, got_ref, core, before(t)))
+    return pairs + singles
 
 
 def near_tiles(cols_ref, near_ref, value_hbm, value_ref, part_ref, table, done):
@@ -187,7 +206,18 @@
 
 
 def tiles(
-    rows_hbm, cols_ref, near_ref, far_ref, part_ref, value_ref, out_ref, rows, table, picked, done
+    rows_hbm,
+    cols_ref,
+    near_ref,
+    far_ref,
+    part_ref,
+    value_ref,
+    out_ref,
+    rows,
+    table,
+    picked,
+    sums_ref,
+    done,
 ):
     copy = pltpu.make_async_copy(rows_hbm, rows, done.at[0])
     copy.start()
@@ -205,32 +235,59 @@
     total = lane_sum(jnp.where((lane >= 67) & (lane < 69), extra, 0.0))
     origin = 8 * ((((lane & 31) >> 2) - lax.axis_index("col")) & 7) + 4 * (lane >> 5) + (lane & 3)
     extra = jnp.take_along_axis(extra, origin & (LANES - 1), axis=1)
-    base = jnp.where(lane < 64, extra, sums + pltpu.roll(sums, 64, 1))
+    sums = sums + pltpu.roll(sums, 64, 1)
+    of_value = exponent(lane_max(jnp.where(lane < 64, extra, 0.0)))
+    of_sum = exponent(lane_max(sums))
+    of_along = exponent(jnp.abs(along))
+    sum_code = code(sums, of_sum)
+    origin = 4 * (lane >> 3) + (lane & 3)
+    upper = jnp.take_along_axis(sum_code >> 8, origin, axis=1)
+    lower = jnp.take_along_axis(sum_code & 255, origin, axis=1)
+    hub_code = jnp.where((lane & 4) == 0, upper, lower)
+    common = jnp.where(lane < 64, code(extra, of_value, 32000.0), 0)
+    along_code = code(along, of_along)
+    total_code = jnp.broadcast_to(total, along.shape).astype(i32)
+    for at, value in (
+        (72, along_code >> 8),
+        (73, along_code & 255),
+        (74, total_code >> 8),
+        (75, total_code & 255),
+        (80, of_value.astype(i32)),
+        (81, of_sum.astype(i32)),
+        (82, of_along.astype(i32)),
+    ):
+        common = jnp.where(lane == at, value, common)
     for s in range(peers):
         for r in range(4):
-            out_ref[s, r] = jnp.zeros((count, LANES), f32)
-        block = jnp.where(lane == 64 + (4 * s + 4) % 64, along, base)
-        out_ref[s, 4] = jnp.where(lane == 64 + (4 * s + 5) % 64, total, block)
+            sums_ref[s, r] = jnp.zeros((count, LANES), f32)
 
     step, twos = 48, 16
 
-    def choose(n):
-        return pick(cols_ref, n * step, step, twos, table, far_ref, 1 - core, lambda t: part_ref[t])
+    def choose(n, beside=lambda: None):
+        return pick(
+            cols_ref, n * step, step, twos, table, far_ref, 1 - core, lambda t: part_ref[t], beside
+        )
+
+    def multiply_some(n, made):
+        def one():
+            t = n * step + len(made)
+            if len(made) < step:
+                left = jnp.concatenate([picked[t], picked[t + 1]], 0)
+                right = jnp.concatenate([value_ref[t], value_ref[t + 1]], 0)
+                both = dot_t(left, right)
+                made.extend([both[:count, :LANES], both[count:, LANES:]])
+        return one
 
     def multiply(n):
         made = []
         for u in range(0, step, 2):
-            t = n * step + u
-            left = jnp.concatenate([picked[t], picked[t + 1]], 0)
-            right = jnp.concatenate([value_ref[t], value_ref[t + 1]], 0)
-            both = dot_t(left, right)
-            made += [both[:count, :LANES], both[count:, LANES:]]
+            multiply_some(n, made)()
         return made
 
     def add(n, made):
         for u in range(step):
             at = rows[n * step + u]
-            out_ref[at >> 2, at & 3] += made[u]
+            sums_ref[at >> 2, at & 3] += made[u]
 
     def keep(n, made):
         for u in range(step):
@@ -240,41 +297,66 @@
     copy.wait()
     steps = part_ref.shape[0] // step
     for n in range(1, steps):
-        products = multiply(n - 1)
-        made = choose(n)
+        products = []
+        made = choose(n, multiply_some(n - 1, products))
+        while len(products) < step:
+            multiply_some(n - 1, products)()
         add(n - 1, products)
         keep(n, made)
     add(steps - 1, multiply(steps - 1))
+    for s in range(peers):
+        blocks = [sums_ref[s, r] for r in range(4)]
+        top = jnp.abs(blocks[0])
+        for r in range(1, 4):
+            top = jnp.maximum(top, jnp.abs(blocks[r]))
+        power = exponent(lane_max(top))
+        codes = [code(block, power) for block in blocks]
+        for r in range(4):
+            out_ref[s, r] = (codes[r] >> 8).astype(jnp.int16)
+        for r in range(2):
+            lower = (codes[2 * r] & 255) + ((codes[2 * r + 1] & 255) << 8)
+            out_ref[s, 4 + r] = (lower - BIAS).astype(jnp.int16)
+        block = jnp.where(lane == 83, power.astype(i32), common)
+        moved = pltpu.roll(hub_code, (64 - 8 * s) % LANES, 1)
+        out_ref[s, 6] = jnp.where((lane >= 64) & (lane < 72), moved, block).astype(jnp.int16)
 
 
 def correct(mark_ref, got_ref, degree_ref, weight_ref, image_ref, out_ref):
-    j = lax.axis_index("col")
     peers, _, count, _ = got_ref.shape
     own, width = mark_ref.shape
     lane = lane_of(count)
     group = (lane & 31) >> 2
+    power_at = jnp.where(lane < 64, 80, jnp.where(lane < 72, 81, jnp.where(lane < 74, 82, 84)))
+    extra = jnp.zeros((count, LANES), f32)
+    blocks = [jnp.zeros((count, LANES), f32)] * 4
+    hub_values = []
+    for s in range(peers):
+        block = got_ref[s, 6].astype(f32)
+        scaled = block * jnp.exp2(jnp.take_along_axis(block, power_at, axis=1))
+        hub_values.append(scaled * (1.0 / 32000.0))
+        extra += scaled
+        unit = jnp.take_along_axis(block, jnp.full((count, LANES), 83, i32), axis=1)
+        unit = jnp.exp2(unit) * (1.0 / UNIT)
+        for r in range(4):
+            lower = got_ref[s, 4 + r // 2].astype(i32) + BIAS
+            lower = lower >> 8 if r % 2 else lower & 255
+            blocks[r] += (got_ref[s, r].astype(i32) * 256 + lower).astype(f32) * unit
     values = []
     for m in range(weight_ref.shape[0] // LANES):
         sides = []
         for first in (0, peers // 2):
-            found = got_ref[first, 4]
+            found = hub_values[first]
             for s in range(first + 1, first + peers // 2):
-                found = jnp.where(group == (m + s) % 8, got_ref[s, 4], found)
+                found = jnp.where(group == (m + s) % 8, hub_values[s], found)
             at = 32 * (lane >> 6) + 4 * ((m + ((lane >> 2) & 7)) & 7) + (lane & 3)
             sides.append(jnp.take_along_axis(found, at, axis=1))
         values.append(jnp.where((lane & 32) == 0, sides[0], sides[1]).astype(bf16))
     hub = jnp.dot(jnp.concatenate(values, 1), weight_ref[...], preferred_element_type=f32)
-    blocks = []
-    for r in range(5):
-        total = got_ref[0, r]
-        for s in range(1, peers):
-            total += got_ref[s, r]
-        blocks.append(total)
-    extra = blocks[4]
-    at_lane = lambda at: lane_sum(jnp.where(lane == at, extra, 0.0))
-    ratio = at_lane(64 + ((4 * j + 4) & 63)) / at_lane(64 + ((4 * j + 5) & 63))
+    at_lane = lambda at: extra[:, at : at + 1]
+    along = (at_lane(72) * 256.0 + at_lane(73)) * (1.0 / UNIT)
+    ratio = along / (at_lane(74) * 256.0 + at_lane(75))
     degrees = degree_ref[...].astype(f32)
-    hub_sum = [at_lane(64 + 4 * j + k) for k in range(own)]
+    hub_sum = [(at_lane(64 + k) * 256.0 + at_lane(68 + k)) * (1.0 / UNIT) for k in range(own)]
     parts = []
     for r in range(width // LANES):
         columns = slice(r * LANES, (r + 1) * LANES)
@@ -355,12 +437,14 @@
             name=name,
         )
 
-    sent, cols, marks = call(
+    sent, cols, marks, degree_rows, weight = call(
         prepare,
         (
             shape((z_n, 7, count, LANES), bf16),
             pltpu.VMEM(tile_cols.shape, i32),
-            shape((own, width), f32),
+            pltpu.VMEM((own, width), f32),
+            pltpu.VMEM(degree_rows.shape, i32),
+            pltpu.VMEM(hub_weight.shape, bf16),
         ),
         [hbm] * 5,
         8,
@@ -368,8 +452,6 @@
         [
             pltpu.SMEM(hub_ids.shape, i32),
             pltpu.VMEM(vectors.shape, bf16),
-            pltpu.VMEM(degree_rows.shape, i32),
-            pltpu.VMEM(hub_weight.shape, bf16),
             pltpu.SemaphoreType.DMA((5,)),
         ],
     )(stay(hub_ids), stay(vectors), stay(degree_rows), stay(hub_weight), stay(tile_cols))
@@ -386,7 +468,7 @@
     )(cols, near, stay(tile_values))
     sent = call(
         tiles,
-        shape((cols_n, 5, count, LANES), f32),
+        shape((cols_n, 7, count, LANES), jnp.int16),
         [hbm, vmem, vmem, vmem, vmem, vmem],
         16,
         "tiles",
@@ -394,6 +476,7 @@
             pltpu.SMEM(tile_rows.shape, i32),
             table,
             pltpu.VMEM((tile_count, count, LANES), bf16),
+            pltpu.VMEM((cols_n, 4, count, LANES), f32),
             pltpu.SemaphoreType.DMA((1,)),
         ],
     )(stay(tile_rows), cols, near, far, part, values)
@@ -404,7 +487,7 @@
         [vmem, vmem, vmem, vmem],
         8,
         "correct",
-    )(marks, got, degree_rows, hub_weight)
+    )(marks, got, degree_rows, weight)
     got = lax.all_to_all(sent, ("z", "core"), 0, 0)
     sent = call(add_up, shape((cols_n, 8, LANES), f32), [vmem], 4, "add_up")(got)
     got = lax.all_to_all(sent, "col", 0, 0)

time: 69.7 us -> 67.6 us (0.970)
  blocking collectives: 58.6 us -> 56.3 us
    all_to_all x2, blocking collectives: 28.6 us -> 26 us  [on_device(): got = lax.all_to_all(sent, 'col', 0, 0)]
where the time goes in v5:
time: 67.6 us; the launch traced here: 67.3 us
  blocking collectives  56.3 us (83%)
  Pallas kernels  7.95 us (12%)
  starting transfers between devices  2.38 us (4%)
    all_to_all x2, blocking collectives, on_device(): got = lax.all_to_all(sent, 'col', 0, 0)  26 us
    all_to_all x1, blocking collectives, on_device(): near = lax.all_to_all(sent, 'z', 0, 0)  18.6 us
    all_to_all x1, blocking collectives, on_device(): got = lax.all_to_all(sent, ('z', 'core'), 0, 0)  11.7 us
    pallas_call x1, Pallas kernels, on_device(): call(tiles, shape((cols_n, 7, count, LANES), jnp.int16), [hbm, vmem, vmem...  2.74 us
    ppermute x1, starting transfers between devices, on_device(): far = lax.ppermute(near, 'core', [(0, 1), (1, 0)])  2.38 us
    pallas_call x1, Pallas kernels, on_device(): call(near_tiles, (pltpu.VMEM(tile_values.shape, bf16), pltpu.VMEM((tile_c...  1.9 us
    pallas_call x1, Pallas kernels, on_device(): call(prepare, (shape((z_n, 7, count, LANES), bf16), pltpu.VMEM(tile_cols....  1.74 us
  transfers between devices with their start and end apart: 1, of which 0 were waited for; matrix products, arithmetic and copies ran while one was open for 0% of the time, Pallas kernels for 3%

profile of v5, /device:TPU:1, one launch (start us, length us, event | category | flops | bytes accessed | tf_op | source)
XLA Modules:
  0.0 67.3 jit_solution(12614094940741388164)
XLA Ops:
  0.6 1.7 %prepare.1 = (bf16[8,7,16,128]{3,2,1,0:T(8,128)(2,1)S(1)}, s32[96,128]{1,0:T(8,128)S(1)}, f32[4,512]{1,0:T(4,128)S(1)}, s32[4,128]{1,0:T(4,128)S(1)}, bf16[1024,512]{1,0:T(8,128)(2,1)S(1)}) custom-call(s32[1024]{0:T(1024)} %ids_hbm.1, bf16[16,512]{1,0:T(8,128)(2,1)} %x_hbm.1, s32[4,128]{1,0:T(4,128)} %bitcast.1, bf16[1024,512]{1,0:T(8,128)(2,1)} %weight_hbm.1, ...), custom_call_target="tpu_custom_call" | custom-call | tf_op jit(solution)/shard_map/prepare/pallas_call | solution.py:440
  2.4 18.6 %all_to_all.20.near_ref = bf16[8,7,16,128]{3,2,1,0:T(8,128)(2,1)S(1)} all-to-all(bf16[8,7,16,128]{3,2,1,0:T(8,128)(2,1)S(1)} %get-tuple-element.13), channel_id=1, replica_groups=mesh['z'=8,'core'=2,'col'=16] {'z'}, dimensions={0} | all-to-all | bytes 458752 | tf_op jit(solution)/shard_map/all_to_all | solution.py:458
  20.9 2.4 %collective-permute-start = (bf16[8,7,16,128]{3,2,1,0:T(8,128)(2,1)S(1)}, bf16[8,7,16,128]{3,2,1,0:T(8,128)(2,1)S(1)}, u32[]{:S(2)}, u32[]{:S(2)}) collective-permute-start(bf16[8,7,16,128]{3,2,1,0:T(8,128)(2,1)S(1)} %all_to_all.20.near_ref), channel_id=1, source_target_pairs={{0,16},{16,0},{1,17},{17,1},{2,18},{18,2},{3,19},{19,3},{4,20},{20... | collective-permute-start | bytes 688136 | tf_op jit(solution)/shard_map/ppermute | solution.py:459
  23.3 1.9 %near_tiles.1 = (bf16[96,128,128]{2,1,0:T(8,128)(2,1)S(1)}, bf16[96,16,128]{2,1,0:T(8,128)(2,1)S(1)}) custom-call(s32[96,128]{1,0:T(8,128)S(1)} %get-tuple-element.12.cols_ref, bf16[8,7,16,128]{3,2,1,0:T(8,128)(2,1)S(1)} %all_to_all.20.near_ref, bf16[96,128,128]{2,1,0:T(8,128)(2,1)} %value_hbm.1), custom_call_target="tpu_custom_call" | custom-call | tf_op jit(solution)/shard_map/near_tiles/pallas_call | solution.py:461
  25.2 0.0 collective-permute-done.far_ref
  25.2 2.7 %tiles.1 = s16[16,7,16,128]{3,2,1,0:T(8,128)(2,1)S(1)} custom-call(s32[96]{0:T(128)} %rows_hbm.1, s32[96,128]{1,0:T(8,128)S(1)} %get-tuple-element.12.cols_ref, bf16[8,7,16,128]{3,2,1,0:T(8,128)(2,1)S(1)} %all_to_all.20.near_ref, bf16[8,7,16,128]{3,2,1,0:T(8,128)(2,1)S(1)} %collective-permute-done.far_ref, ...), custom_call_target="tpu_custom_call" | custom-call | tf_op jit(solution)/shard_map/tiles/pallas_call | solution.py:469
  28.0 16.9 %all_to_all.21.got_ref = s16[16,7,16,128]{3,2,1,0:T(8,128)(2,1)S(1)} all-to-all(s16[16,7,16,128]{3,2,1,0:T(8,128)(2,1)S(1)} %tiles.1), channel_id=1, replica_groups=mesh['z'=8,'core'=2,'col'=16] {'col'}, dimensions={0} | all-to-all | bytes 917504 | tf_op jit(solution)/shard_map/all_to_all | solution.py:483
  44.9 0.6 correct.1
  45.5 11.7 %all_to_all.22.got_ref = f32[16,8,128]{2,1,0:T(8,128)S(1)} all-to-all(f32[16,8,128]{2,1,0:T(8,128)S(1)} %get-tuple-element.18), channel_id=1, replica_groups=mesh['z'=8,'core'=2,'col'=16] {'z','core'}, dimensions={0} | all-to-all | bytes 131072 | tf_op jit(solution)/shard_map/all_to_all | solution.py:491
  57.3 9.1 %all_to_all.23.got_ref = f32[16,8,128]{2,1,0:T(8,128)S(1)} all-to-all(f32[16,8,128]{2,1,0:T(8,128)S(1)} %add_up.1), channel_id=1, replica_groups=mesh['z'=8,'core'=2,'col'=16] {'col'}, dimensions={0} | all-to-all | bytes 131072 | tf_op jit(solution)/shard_map/all_to_all | solution.py:493
  66.4 0.9 %finish.1 = (f32[16,512]{1,0:T(8,128)}, f32[16,16]{1,0:T(8,128)}) custom-call(f32[16,8,128]{2,1,0:T(8,128)S(1)} %all_to_all.23.got_ref, f32[16,512]{1,0:T(8,128)S(1)} %get-tuple-element.19.image_ref), custom_call_target="tpu_custom_call" | custom-call | tf_op jit(solution)/shard_map/finish/pallas_call | solution.py:494
  (1 shorter events, 0.0 us)
Async XLA Ops:
  20.9 4.3 %collective-permute-start = (bf16[8,7,16,128]{3,2,1,0:T(8,128)(2,1)S(1)}, bf16[8,7,16,128]{3,2,1,0:T(8,128)(2,1)S(1)}, u32[]{:S(2)}, u32[]{:S(2)}) collective-permute-start(bf16[8,7,16,128]{3,2,1,0:T(8,128)(2,1)S(1)} %all_to_all.20.near_ref), channel_id=1, source_target_pairs={{0,16},{16,0},{1,17},{17,1},{2,18},{18,2},{3,19},{19,3},{4,20},{20... | collective-permute-start | bytes 688136 | tf_op jit(solution)/shard_map/ppermute | solution.py:459

commit v6 on v5

--- a/solution.py
+++ b/solution.py
@@ -37,6 +37,7 @@
 
 
 UNIT = 8300000.0
+SHORT_UNIT = 520000.0
 BIAS = 32768
 
 
@@ -58,11 +59,13 @@
     degree_hbm,
     weight_hbm,
     cols_hbm,
+    value_hbm,
     out_ref,
     cols_ref,
     mark_ref,
     degree_ref,
     weight_ref,
+    value_ref,
     ids,
     x_ref,
     done,
@@ -73,6 +76,7 @@
         (degree_hbm, degree_ref),
         (ids_hbm, ids),
         (cols_hbm, cols_ref),
+        (value_hbm.at[pl.ds(0, value_ref.shape[0])], value_ref),
     )
     copies = [pltpu.make_async_copy(a, b, done.at[n]) for n, (a, b) in enumerate(pairs)]
     for copy in copies:
@@ -114,7 +118,8 @@
         odd = jnp.where(lane < 64, pltpu.roll(head, 64, 1), tail)
         out_ref[s, 4] = even.astype(bf16)
         out_ref[s, 5] = odd.astype(bf16)
-    copies[-1].wait()
+    copies[4].wait()
+    copies[5].wait()
 
 
 def fill(table, got_ref):
@@ -188,7 +193,9 @@
 
 
 def near_tiles(cols_ref, near_ref, value_hbm, value_ref, part_ref, table, done):
-    copy = pltpu.make_async_copy(value_hbm, value_ref, done.at[0])
+    late = value_ref.shape[0]
+    source = value_hbm.at[pl.ds(value_hbm.shape[0] - late, late)]
+    copy = pltpu.make_async_copy(source, value_ref, done.at[0])
     copy.start()
     core = lax.axis_index("core")
     fill(table, near_ref)
@@ -211,6 +218,7 @@
     near_ref,
     far_ref,
     part_ref,
+    first_ref,
     value_ref,
     out_ref,
     rows,
@@ -262,6 +270,8 @@
             sums_ref[s, r] = jnp.zeros((count, LANES), f32)
 
     step, twos = 48, 16
+    early = first_ref.shape[0]
+    value = lambda t: first_ref[t] if t < early else value_ref[t - early]
 
     def choose(n, beside=lambda: None):
         return pick(
@@ -273,7 +283,7 @@
             t = n * step + len(made)
             if len(made) < step:
                 left = jnp.concatenate([picked[t], picked[t + 1]], 0)
-                right = jnp.concatenate([value_ref[t], value_ref[t + 1]], 0)
+                right = jnp.concatenate([value(t), value(t + 1)], 0)
                 both = dot_t(left, right)
                 made.extend([both[:count, :LANES], both[count:, LANES:]])
         return one
@@ -310,15 +320,15 @@
         for r in range(1, 4):
             top = jnp.maximum(top, jnp.abs(blocks[r]))
         power = exponent(lane_max(top))
-        codes = [code(block, power) for block in blocks]
+        lower = jnp.full((count, LANES), -BIAS, i32)
         for r in range(4):
-            out_ref[s, r] = (codes[r] >> 8).astype(jnp.int16)
-        for r in range(2):
-            lower = (codes[2 * r] & 255) + ((codes[2 * r + 1] & 255) << 8)
-            out_ref[s, 4 + r] = (lower - BIAS).astype(jnp.int16)
+            number = code(blocks[r], power, SHORT_UNIT)
+            out_ref[s, r] = (number >> 4).astype(jnp.int16)
+            lower += (number & 15) << (4 * r)
+        out_ref[s, 4] = lower.astype(jnp.int16)
         block = jnp.where(lane == 83, power.astype(i32), common)
         moved = pltpu.roll(hub_code, (64 - 8 * s) % LANES, 1)
-        out_ref[s, 6] = jnp.where((lane >= 64) & (lane < 72), moved, block).astype(jnp.int16)
+        out_ref[s, 5] = jnp.where((lane >= 64) & (lane < 72), moved, block).astype(jnp.int16)
 
 
 def correct(mark_ref, got_ref, degree_ref, weight_ref, image_ref, out_ref):
@@ -331,16 +341,16 @@
     blocks = [jnp.zeros((count, LANES), f32)] * 4
     hub_values = []
     for s in range(peers):
-        block = got_ref[s, 6].astype(f32)
+        block = got_ref[s, 5].astype(f32)
         scaled = block * jnp.exp2(jnp.take_along_axis(block, power_at, axis=1))
         hub_values.append(scaled * (1.0 / 32000.0))
         extra += scaled
         unit = jnp.take_along_axis(block, jnp.full((count, LANES), 83, i32), axis=1)
-        unit = jnp.exp2(unit) * (1.0 / UNIT)
+        unit = jnp.exp2(unit) * (1.0 / SHORT_UNIT)
+        lower = got_ref[s, 4].astype(i32) + BIAS
         for r in range(4):
-            lower = got_ref[s, 4 + r // 2].astype(i32) + BIAS
-            lower = lower >> 8 if r % 2 else lower & 255
-            blocks[r] += (got_ref[s, r].astype(i32) * 256 + lower).astype(f32) * unit
+            number = got_ref[s, r].astype(i32) * 16 + ((lower >> (4 * r)) & 15)
+            blocks[r] += number.astype(f32) * unit
     values = []
     for m in range(weight_ref.shape[0] // LANES):
         sides = []
@@ -418,6 +428,7 @@
     rows_n = 2 * z_n
     tile_count = tile_values.shape[0]
     own = hub_ids.shape[0] // (rows_n * cols_n)
+    early = tile_count // 3
     vmem = pl.BlockSpec(memory_space=pltpu.VMEM)
     hbm = pl.BlockSpec(memory_space=pltpu.HBM)
     shape = jax.ShapeDtypeStruct
@@ -437,7 +448,7 @@
             name=name,
         )
 
-    sent, cols, marks, degree_rows, weight = call(
+    sent, cols, marks, degree_rows, weight, first_values = call(
         prepare,
         (
             shape((z_n, 7, count, LANES), bf16),
@@ -445,22 +456,33 @@
             pltpu.VMEM((own, width), f32),
             pltpu.VMEM(degree_rows.shape, i32),
             pltpu.VMEM(hub_weight.shape, bf16),
+            pltpu.VMEM((early, LANES, LANES), bf16),
         ),
-        [hbm] * 5,
+        [hbm] * 6,
         8,
         "prepare",
         [
             pltpu.SMEM(hub_ids.shape, i32),
             pltpu.VMEM(vectors.shape, bf16),
-            pltpu.SemaphoreType.DMA((5,)),
+            pltpu.SemaphoreType.DMA((6,)),
         ],
-    )(stay(hub_ids), stay(vectors), stay(degree_rows), stay(hub_weight), stay(tile_cols))
+    )(
+        stay(hub_ids),
+        stay(vectors),
+        stay(degree_rows),
+        stay(hub_weight),
+        stay(tile_cols),
+        stay(tile_values),
+    )
     near = lax.all_to_all(sent, "z", 0, 0)
     far = lax.ppermute(near, "core", [(0, 1), (1, 0)])
     table = pltpu.VMEM((rows_n * count, 2 * LANES), bf16)
     values, part = call(
         near_tiles,
-        (pltpu.VMEM(tile_values.shape, bf16), pltpu.VMEM((tile_count, count, LANES), bf16)),
+        (
+            pltpu.VMEM((tile_count - early, LANES, LANES), bf16),
+            pltpu.VMEM((tile_count, count, LANES), bf16),
+        ),
         [vmem, vmem, hbm],
         16,
         "near_tiles",
@@ -468,8 +490,8 @@
     )(cols, near, stay(tile_values))
     sent = call(
         tiles,
-        shape((cols_n, 7, count, LANES), jnp.int16),
-        [hbm, vmem, vmem, vmem, vmem, vmem],
+        shape((cols_n, 6, count, LANES), jnp.int16),
+        [hbm] + [vmem] * 6,
         16,
         "tiles",
         [
@@ -479,7 +501,7 @@
             pltpu.VMEM((cols_n, 4, count, LANES), f32),
             pltpu.SemaphoreType.DMA((1,)),
         ],
-    )(stay(tile_rows), cols, near, far, part, values)
+    )(stay(tile_rows), cols, near, far, part, first_values, values)
     got = lax.all_to_all(sent, "col", 0, 0)
     image, sent = call(
         correct,

time: 67.6 us -> 66.6 us (0.985)
  blocking collectives: 56.3 us -> 55.6 us
    all_to_all x2, blocking collectives: 26 us -> 25.3 us  [on_device(): got = lax.all_to_all(sent, 'col', 0, 0)]
  transfers between devices with their start and end apart: 1 -> 1, of which waited for: 0 -> 0; matrix products, arithmetic and copies ran while one was open for 0% -> 0% of each run, Pallas kernels for 3% -> 2%
where the time goes in v6:
time: 66.6 us; the launch traced here: 66.3 us
  blocking collectives  55.6 us (83%)
  Pallas kernels  7.65 us (11%)
  starting transfers between devices  2.38 us (4%)
  between operations  0.67 us (1%)
    all_to_all x2, blocking collectives, on_device(): got = lax.all_to_all(sent, 'col', 0, 0)  25.3 us
    all_to_all x1, blocking collectives, on_device(): near = lax.all_to_all(sent, 'z', 0, 0)  18.6 us
    all_to_all x1, blocking collectives, on_device(): got = lax.all_to_all(sent, ('z', 'core'), 0, 0)  11.7 us
    pallas_call x1, Pallas kernels, on_device(): call(tiles, shape((cols_n, 6, count, LANES), jnp.int16), [hbm] + [vmem] *...  2.73 us
    ppermute x1, starting transfers between devices, on_device(): far = lax.ppermute(near, 'core', [(0, 1), (1, 0)])  2.38 us
    pallas_call x1, Pallas kernels, on_device(): call(prepare, (shape((z_n, 7, count, LANES), bf16), pltpu.VMEM(tile_cols....  1.75 us
    pallas_call x1, Pallas kernels, on_device(): call(near_tiles, (pltpu.VMEM((tile_count - early, LANES, LANES), bf16), p...  1.6 us
  transfers between devices with their start and end apart: 1, of which 0 were waited for; matrix products, arithmetic and copies ran while one was open for 0% of the time, Pallas kernels for 2%

profile of v6, /device:TPU:1, one launch (start us, length us, event | category | flops | bytes accessed | tf_op | source)
XLA Modules:
  0.0 66.3 jit_solution(17969085628379575517)
XLA Ops:
  0.6 1.8 %prepare.1 = (bf16[8,7,16,128]{3,2,1,0:T(8,128)(2,1)S(1)}, s32[96,128]{1,0:T(8,128)S(1)}, f32[4,512]{1,0:T(4,128)S(1)}, s32[4,128]{1,0:T(4,128)S(1)}, bf16[1024,...) custom-call(s32[1024]{0:T(1024)} %ids_hbm.1, bf16[16,512]{1,0:T(8,128)(2,1)} %x_hbm.1, s32[4,128]{1,0:T(4,128)} %bitcast.1, ...), custom_call_target="tpu_custom_call" | custom-call | tf_op jit(solution)/shard_map/prepare/pallas_call | solution.py:451
  2.4 18.6 %all_to_all.20.near_ref = bf16[8,7,16,128]{3,2,1,0:T(8,128)(2,1)S(1)} all-to-all(bf16[8,7,16,128]{3,2,1,0:T(8,128)(2,1)S(1)} %get-tuple-element.14), channel_id=1, replica_groups=mesh['z'=8,'core'=2,'col'=16] {'z'}, dimensions={0} | all-to-all | bytes 458752 | tf_op jit(solution)/shard_map/all_to_all | solution.py:477
  21.0 2.4 %collective-permute-start = (bf16[8,7,16,128]{3,2,1,0:T(8,128)(2,1)S(1)}, bf16[8,7,16,128]{3,2,1,0:T(8,128)(2,1)S(1)}, u32[]{:S(2)}, u32[]{:S(2)}) collective-permute-start(bf16[8,7,16,128]{3,2,1,0:T(8,128)(2,1)S(1)} %all_to_all.20.near_ref), channel_id=1, source_target_pairs={{0,16},{16,0},{1,17},{17,1},{2,18},{18,2},{3,19},{19,3},{4,20},{20... | collective-permute-start | bytes 688136 | tf_op jit(solution)/shard_map/ppermute | solution.py:478
  23.3 1.6 %near_tiles.1 = (bf16[64,128,128]{2,1,0:T(8,128)(2,1)S(1)}, bf16[96,16,128]{2,1,0:T(8,128)(2,1)S(1)}) custom-call(s32[96,128]{1,0:T(8,128)S(1)} %get-tuple-element.13.cols_ref, bf16[8,7,16,128]{3,2,1,0:T(8,128)(2,1)S(1)} %all_to_all.20.near_ref, bf16[96,128,128]{2,1,0:T(8,128)(2,1)} %value_hbm.3), custom_call_target="tpu_custom_call" | custom-call | tf_op jit(solution)/shard_map/near_tiles/pallas_call | solution.py:480
  24.9 0.0 collective-permute-done.far_ref
  25.0 2.7 %tiles.1 = s16[16,6,16,128]{3,2,1,0:T(8,128)(2,1)S(1)} custom-call(s32[96]{0:T(128)} %rows_hbm.1, s32[96,128]{1,0:T(8,128)S(1)} %get-tuple-element.13.cols_ref, bf16[8,7,16,128]{3,2,1,0:T(8,128)(2,1)S(1)} %all_to_all.20.near_ref, bf16[8,7,16,128]{3,2,1,0:T(8,128)(2,1)S(1)} %collective-permute-done.far_ref, ...), custom_call_target="tpu_custom_call" | custom-call | tf_op jit(solution)/shard_map/tiles/pallas_call | solution.py:491
  27.7 16.2 %all_to_all.21.got_ref = s16[16,6,16,128]{3,2,1,0:T(8,128)(2,1)S(1)} all-to-all(s16[16,6,16,128]{3,2,1,0:T(8,128)(2,1)S(1)} %tiles.1), channel_id=1, replica_groups=mesh['z'=8,'core'=2,'col'=16] {'col'}, dimensions={0} | all-to-all | bytes 786432 | tf_op jit(solution)/shard_map/all_to_all | solution.py:505
  43.9 0.6 correct.1
  44.5 11.7 %all_to_all.22.got_ref = f32[16,8,128]{2,1,0:T(8,128)S(1)} all-to-all(f32[16,8,128]{2,1,0:T(8,128)S(1)} %get-tuple-element.20), channel_id=1, replica_groups=mesh['z'=8,'core'=2,'col'=16] {'z','core'}, dimensions={0} | all-to-all | bytes 131072 | tf_op jit(solution)/shard_map/all_to_all | solution.py:513
  56.2 9.1 %all_to_all.23.got_ref = f32[16,8,128]{2,1,0:T(8,128)S(1)} all-to-all(f32[16,8,128]{2,1,0:T(8,128)S(1)} %add_up.1), channel_id=1, replica_groups=mesh['z'=8,'core'=2,'col'=16] {'col'}, dimensions={0} | all-to-all | bytes 131072 | tf_op jit(solution)/shard_map/all_to_all | solution.py:515
  65.3 0.9 %finish.1 = (f32[16,512]{1,0:T(8,128)}, f32[16,16]{1,0:T(8,128)}) custom-call(f32[16,8,128]{2,1,0:T(8,128)S(1)} %all_to_all.23.got_ref, f32[16,512]{1,0:T(8,128)S(1)} %get-tuple-element.21.image_ref), custom_call_target="tpu_custom_call" | custom-call | tf_op jit(solution)/shard_map/finish/pallas_call | solution.py:516
  (1 shorter events, 0.0 us)
Async XLA Ops:
  21.0 4.0 %collective-permute-start = (bf16[8,7,16,128]{3,2,1,0:T(8,128)(2,1)S(1)}, bf16[8,7,16,128]{3,2,1,0:T(8,128)(2,1)S(1)}, u32[]{:S(2)}, u32[]{:S(2)}) collective-permute-start(bf16[8,7,16,128]{3,2,1,0:T(8,128)(2,1)S(1)} %all_to_all.20.near_ref), channel_id=1, source_target_pairs={{0,16},{16,0},{1,17},{17,1},{2,18},{18,2},{3,19},{19,3},{4,20},{20... | collective-permute-start | bytes 688136 | tf_op jit(solution)/shard_map/ppermute | solution.py:478

commit v7 on v6

--- a/solution.py
+++ b/solution.py
@@ -114,10 +114,8 @@
     part = dot_t(x, weight_ref[...])
     for s in range(peers):
         head, tail = pieces(part[:, s * LANES : (s + 1) * LANES], 2)
-        even = jnp.where(lane < 64, head, pltpu.roll(tail, 64, 1))
-        odd = jnp.where(lane < 64, pltpu.roll(head, 64, 1), tail)
-        out_ref[s, 4] = even.astype(bf16)
-        out_ref[s, 5] = odd.astype(bf16)
+        out_ref[s, 4] = head.astype(bf16)
+        out_ref[s, 5] = tail.astype(bf16)
     copies[4].wait()
     copies[5].wait()
 
@@ -141,7 +139,7 @@
     found = jnp.dot(table[...], jnp.concatenate(hot, 1), preferred_element_type=f32)
     count = before[0].shape[0]
     for e in range(2):
-        halves = [before[e][q * 8 : q * 8 + 8].astype(f32) for q in range(2)]
+        halves = [before[e].astype(f32)[q * 8 : q * 8 + 8] for q in range(2)]
         for h in range(table.shape[0] // count):
             mask = high[e] == (h // 2) * 4 + h % 2
             for q in range(2):
@@ -237,13 +235,14 @@
     extra = jnp.zeros((count, LANES), f32)
     for got_ref in (near_ref, far_ref):
         for z in range(got_ref.shape[0]):
-            sums += got_ref[z, 4 + core].astype(f32)
+            sums += got_ref[z, 4].astype(f32) + got_ref[z, 5].astype(f32)
             extra += got_ref[z, 6].astype(f32)
     along = lane_sum(jnp.where((lane >= 64) & (lane < 67), extra, 0.0))
     total = lane_sum(jnp.where((lane >= 67) & (lane < 69), extra, 0.0))
     origin = 8 * ((((lane & 31) >> 2) - lax.axis_index("col")) & 7) + 4 * (lane >> 5) + (lane & 3)
     extra = jnp.take_along_axis(extra, origin & (LANES - 1), axis=1)
-    sums = sums + pltpu.roll(sums, 64, 1)
+    sums = jnp.where(core == 0, sums, pltpu.roll(sums, 64, 1))
+    sums = jnp.where(lane < 64, sums, 0.0)
     of_value = exponent(lane_max(jnp.where(lane < 64, extra, 0.0)))
     of_sum = exponent(lane_max(sums))
     of_along = exponent(jnp.abs(along))

time: 66.6 us -> 66.5 us (level)
  no operation moved by 1% of the time
where the time goes in v7:
time: 66.5 us; the launch traced here: 66.2 us
  blocking collectives  55.6 us (84%)
  Pallas kernels  7.57 us (11%)
  starting transfers between devices  2.38 us (4%)
  between operations  0.67 us (1%)
    all_to_all x2, blocking collectives, on_device(): got = lax.all_to_all(sent, 'col', 0, 0)  25.3 us
    all_to_all x1, blocking collectives, on_device(): near = lax.all_to_all(sent, 'z', 0, 0)  18.6 us
    all_to_all x1, blocking collectives, on_device(): got = lax.all_to_all(sent, ('z', 'core'), 0, 0)  11.7 us
    pallas_call x1, Pallas kernels, on_device(): call(tiles, shape((cols_n, 6, count, LANES), jnp.int16), [hbm] + [vmem] *...  2.73 us
    ppermute x1, starting transfers between devices, on_device(): far = lax.ppermute(near, 'core', [(0, 1), (1, 0)])  2.38 us
    pallas_call x1, Pallas kernels, on_device(): call(prepare, (shape((z_n, 7, count, LANES), bf16), pltpu.VMEM(tile_cols....  1.68 us
    pallas_call x1, Pallas kernels, on_device(): call(near_tiles, (pltpu.VMEM((tile_count - early, LANES, LANES), bf16), p...  1.6 us
  transfers between devices with their start and end apart: 1, of which 0 were waited for; matrix products, arithmetic and copies ran while one was open for 0% of the time, Pallas kernels for 2%

profile of v7, /device:TPU:1, one launch (start us, length us, event | category | flops | bytes accessed | tf_op | source)
XLA Modules:
  0.0 66.2 jit_solution(12125084572378342749)
XLA Ops:
  0.6 1.7 %prepare.1 = (bf16[8,7,16,128]{3,2,1,0:T(8,128)(2,1)S(1)}, s32[96,128]{1,0:T(8,128)S(1)}, f32[4,512]{1,0:T(4,128)S(1)}, s32[4,128]{1,0:T(4,128)S(1)}, bf16[1024,...) custom-call(s32[1024]{0:T(1024)} %ids_hbm.1, bf16[16,512]{1,0:T(8,128)(2,1)} %x_hbm.1, s32[4,128]{1,0:T(4,128)} %bitcast.1, ...), custom_call_target="tpu_custom_call" | custom-call | tf_op jit(solution)/shard_map/prepare/pallas_call | solution.py:450
  2.3 18.6 %all_to_all.20.near_ref = bf16[8,7,16,128]{3,2,1,0:T(8,128)(2,1)S(1)} all-to-all(bf16[8,7,16,128]{3,2,1,0:T(8,128)(2,1)S(1)} %get-tuple-element.14), channel_id=1, replica_groups=mesh['z'=8,'core'=2,'col'=16] {'z'}, dimensions={0} | all-to-all | bytes 458752 | tf_op jit(solution)/shard_map/all_to_all | solution.py:476
  20.9 2.4 %collective-permute-start = (bf16[8,7,16,128]{3,2,1,0:T(8,128)(2,1)S(1)}, bf16[8,7,16,128]{3,2,1,0:T(8,128)(2,1)S(1)}, u32[]{:S(2)}, u32[]{:S(2)}) collective-permute-start(bf16[8,7,16,128]{3,2,1,0:T(8,128)(2,1)S(1)} %all_to_all.20.near_ref), channel_id=1, source_target_pairs={{0,16},{16,0},{1,17},{17,1},{2,18},{18,2},{3,19},{19,3},{4,20},{20... | collective-permute-start | bytes 688136 | tf_op jit(solution)/shard_map/ppermute | solution.py:477
  23.3 1.6 %near_tiles.1 = (bf16[64,128,128]{2,1,0:T(8,128)(2,1)S(1)}, bf16[96,16,128]{2,1,0:T(8,128)(2,1)S(1)}) custom-call(s32[96,128]{1,0:T(8,128)S(1)} %get-tuple-element.13.cols_ref, bf16[8,7,16,128]{3,2,1,0:T(8,128)(2,1)S(1)} %all_to_all.20.near_ref, bf16[96,128,128]{2,1,0:T(8,128)(2,1)} %value_hbm.3), custom_call_target="tpu_custom_call" | custom-call | tf_op jit(solution)/shard_map/near_tiles/pallas_call | solution.py:479
  24.9 0.0 collective-permute-done.far_ref
  24.9 2.7 %tiles.1 = s16[16,6,16,128]{3,2,1,0:T(8,128)(2,1)S(1)} custom-call(s32[96]{0:T(128)} %rows_hbm.1, s32[96,128]{1,0:T(8,128)S(1)} %get-tuple-element.13.cols_ref, bf16[8,7,16,128]{3,2,1,0:T(8,128)(2,1)S(1)} %all_to_all.20.near_ref, bf16[8,7,16,128]{3,2,1,0:T(8,128)(2,1)S(1)} %collective-permute-done.far_ref, ...), custom_call_target="tpu_custom_call" | custom-call | tf_op jit(solution)/shard_map/tiles/pallas_call | solution.py:490
  27.6 16.2 %all_to_all.21.got_ref = s16[16,6,16,128]{3,2,1,0:T(8,128)(2,1)S(1)} all-to-all(s16[16,6,16,128]{3,2,1,0:T(8,128)(2,1)S(1)} %tiles.1), channel_id=1, replica_groups=mesh['z'=8,'core'=2,'col'=16] {'col'}, dimensions={0} | all-to-all | bytes 786432 | tf_op jit(solution)/shard_map/all_to_all | solution.py:504
  43.8 0.6 correct.1
  44.4 11.7 %all_to_all.22.got_ref = f32[16,8,128]{2,1,0:T(8,128)S(1)} all-to-all(f32[16,8,128]{2,1,0:T(8,128)S(1)} %get-tuple-element.20), channel_id=1, replica_groups=mesh['z'=8,'core'=2,'col'=16] {'z','core'}, dimensions={0} | all-to-all | bytes 131072 | tf_op jit(solution)/shard_map/all_to_all | solution.py:512
  56.2 9.1 %all_to_all.23.got_ref = f32[16,8,128]{2,1,0:T(8,128)S(1)} all-to-all(f32[16,8,128]{2,1,0:T(8,128)S(1)} %add_up.1), channel_id=1, replica_groups=mesh['z'=8,'core'=2,'col'=16] {'col'}, dimensions={0} | all-to-all | bytes 131072 | tf_op jit(solution)/shard_map/all_to_all | solution.py:514
  65.3 0.9 %finish.1 = (f32[16,512]{1,0:T(8,128)}, f32[16,16]{1,0:T(8,128)}) custom-call(f32[16,8,128]{2,1,0:T(8,128)S(1)} %all_to_all.23.got_ref, f32[16,512]{1,0:T(8,128)S(1)} %get-tuple-element.21.image_ref), custom_call_target="tpu_custom_call" | custom-call | tf_op jit(solution)/shard_map/finish/pallas_call | solution.py:515
  (1 shorter events, 0.0 us)
Async XLA Ops:
  20.9 4.0 %collective-permute-start = (bf16[8,7,16,128]{3,2,1,0:T(8,128)(2,1)S(1)}, bf16[8,7,16,128]{3,2,1,0:T(8,128)(2,1)S(1)}, u32[]{:S(2)}, u32[]{:S(2)}) collective-permute-start(bf16[8,7,16,128]{3,2,1,0:T(8,128)(2,1)S(1)} %all_to_all.20.near_ref), channel_id=1, source_target_pairs={{0,16},{16,0},{1,17},{17,1},{2,18},{18,2},{3,19},{19,3},{4,20},{20... | collective-permute-start | bytes 688136 | tf_op jit(solution)/shard_map/ppermute | solution.py:477

commit v8 on v7

--- a/solution.py
+++ b/solution.py
@@ -376,7 +376,11 @@
         image_ref[:, columns] = parts[r]
     image = jnp.concatenate(parts, 1)
     gram = dot_t(image, image, lax.Precision.HIGHEST)
-    packed = jnp.concatenate([gram[0:8], gram[8:16], jnp.zeros((8, LANES - 32), f32)], 1)
+    spread = jnp.concatenate([gram] * (LANES // count), 1)
+    row = lax.broadcasted_iota(i32, (count, LANES), 0)
+    spread = jnp.where(lane >> 4 == (row & 7), spread, 0.0)
+    packed = [jnp.sum(spread[h : h + 8], axis=0, keepdims=True) for h in (0, 8)]
+    packed = jnp.concatenate(packed, 0)
     for s in range(out_ref.shape[0]):
         out_ref[s] = packed
 
@@ -395,7 +399,9 @@
         total += got_ref[s]
     total = total * scale
     count, width = image_ref.shape
-    left = jnp.concatenate([total, pltpu.roll(total, LANES - 16, 1)], 0)
+    at = 16 * lax.broadcasted_iota(i32, (8, LANES), 0) + (lane_of(8) & 15)
+    halves = [jnp.broadcast_to(total[h : h + 1], (8, LANES)) for h in range(2)]
+    left = jnp.concatenate([jnp.take_along_axis(half, at, axis=1) for half in halves], 0)
     image = image_ref[...]
     lane = lane_of(count)
     row = lax.broadcasted_iota(i32, (count, LANES), 0)
@@ -504,13 +510,13 @@
     got = lax.all_to_all(sent, "col", 0, 0)
     image, sent = call(
         correct,
-        (shape((count, width), f32), shape((rows_n, 8, LANES), f32)),
+        (shape((count, width), f32), shape((rows_n, 2, LANES), f32)),
         [vmem, vmem, vmem, vmem],
         8,
         "correct",
     )(marks, got, degree_rows, weight)
     got = lax.all_to_all(sent, ("z", "core"), 0, 0)
-    sent = call(add_up, shape((cols_n, 8, LANES), f32), [vmem], 4, "add_up")(got)
+    sent = call(add_up, shape((cols_n, 2, LANES), f32), [vmem], 4, "add_up")(got)
     got = lax.all_to_all(sent, "col", 0, 0)
     return call(
         functools.partial(finish, 1.0 / (width * rows_n * cols_n)),

time: 66.5 us -> 66.1 us (level)
  no operation moved by 1% of the time
where the time goes in v8:
time: 66.1 us; the launch traced here: 65.8 us
  blocking collectives  55 us (83%)
  Pallas kernels  7.76 us (12%)
  starting transfers between devices  2.38 us (4%)
  between operations  0.67 us (1%)
    all_to_all x2, blocking collectives, on_device(): got = lax.all_to_all(sent, 'col', 0, 0)  25.2 us
    all_to_all x1, blocking collectives, on_device(): near = lax.all_to_all(sent, 'z', 0, 0)  18.6 us
    all_to_all x1, blocking collectives, on_device(): got = lax.all_to_all(sent, ('z', 'core'), 0, 0)  11.2 us
    pallas_call x1, Pallas kernels, on_device(): call(tiles, shape((cols_n, 6, count, LANES), jnp.int16), [hbm] + [vmem] *...  2.73 us
    ppermute x1, starting transfers between devices, on_device(): far = lax.ppermute(near, 'core', [(0, 1), (1, 0)])  2.38 us
    pallas_call x1, Pallas kernels, on_device(): call(prepare, (shape((z_n, 7, count, LANES), bf16), pltpu.VMEM(tile_cols....  1.68 us
    pallas_call x1, Pallas kernels, on_device(): call(near_tiles, (pltpu.VMEM((tile_count - early, LANES, LANES), bf16), p...  1.6 us
  transfers between devices with their start and end apart: 1, of which 0 were waited for; matrix products, arithmetic and copies ran while one was open for 0% of the time, Pallas kernels for 2%

profile of v8, /device:TPU:1, one launch (start us, length us, event | category | flops | bytes accessed | tf_op | source)
XLA Modules:
  0.0 65.8 jit_solution(6210231895527197110)
XLA Ops:
  0.6 1.7 %prepare.1 = (bf16[8,7,16,128]{3,2,1,0:T(8,128)(2,1)S(1)}, s32[96,128]{1,0:T(8,128)S(1)}, f32[4,512]{1,0:T(4,128)S(1)}, s32[4,128]{1,0:T(4,128)S(1)}, bf16[1024,...) custom-call(s32[1024]{0:T(1024)} %ids_hbm.1, bf16[16,512]{1,0:T(8,128)(2,1)} %x_hbm.1, s32[4,128]{1,0:T(4,128)} %bitcast.1, ...), custom_call_target="tpu_custom_call" | custom-call | tf_op jit(solution)/shard_map/prepare/pallas_call | solution.py:456
  2.3 18.6 %all_to_all.20.near_ref = bf16[8,7,16,128]{3,2,1,0:T(8,128)(2,1)S(1)} all-to-all(bf16[8,7,16,128]{3,2,1,0:T(8,128)(2,1)S(1)} %get-tuple-element.14), channel_id=1, replica_groups=mesh['z'=8,'core'=2,'col'=16] {'z'}, dimensions={0} | all-to-all | bytes 458752 | tf_op jit(solution)/shard_map/all_to_all | solution.py:482
  20.9 2.4 %collective-permute-start = (bf16[8,7,16,128]{3,2,1,0:T(8,128)(2,1)S(1)}, bf16[8,7,16,128]{3,2,1,0:T(8,128)(2,1)S(1)}, u32[]{:S(2)}, u32[]{:S(2)}) collective-permute-start(bf16[8,7,16,128]{3,2,1,0:T(8,128)(2,1)S(1)} %all_to_all.20.near_ref), channel_id=1, source_target_pairs={{0,16},{16,0},{1,17},{17,1},{2,18},{18,2},{3,19},{19,3},{4,20},{20... | collective-permute-start | bytes 688136 | tf_op jit(solution)/shard_map/ppermute | solution.py:483
  23.3 1.6 %near_tiles.1 = (bf16[64,128,128]{2,1,0:T(8,128)(2,1)S(1)}, bf16[96,16,128]{2,1,0:T(8,128)(2,1)S(1)}) custom-call(s32[96,128]{1,0:T(8,128)S(1)} %get-tuple-element.13.cols_ref, bf16[8,7,16,128]{3,2,1,0:T(8,128)(2,1)S(1)} %all_to_all.20.near_ref, bf16[96,128,128]{2,1,0:T(8,128)(2,1)} %value_hbm.3), custom_call_target="tpu_custom_call" | custom-call | tf_op jit(solution)/shard_map/near_tiles/pallas_call | solution.py:485
  24.9 0.0 collective-permute-done.far_ref
  24.9 2.7 %tiles.1 = s16[16,6,16,128]{3,2,1,0:T(8,128)(2,1)S(1)} custom-call(s32[96]{0:T(128)} %rows_hbm.1, s32[96,128]{1,0:T(8,128)S(1)} %get-tuple-element.13.cols_ref, bf16[8,7,16,128]{3,2,1,0:T(8,128)(2,1)S(1)} %all_to_all.20.near_ref, bf16[8,7,16,128]{3,2,1,0:T(8,128)(2,1)S(1)} %collective-permute-done.far_ref, ...), custom_call_target="tpu_custom_call" | custom-call | tf_op jit(solution)/shard_map/tiles/pallas_call | solution.py:496
  27.6 16.2 %all_to_all.21.got_ref = s16[16,6,16,128]{3,2,1,0:T(8,128)(2,1)S(1)} all-to-all(s16[16,6,16,128]{3,2,1,0:T(8,128)(2,1)S(1)} %tiles.1), channel_id=1, replica_groups=mesh['z'=8,'core'=2,'col'=16] {'col'}, dimensions={0} | all-to-all | bytes 786432 | tf_op jit(solution)/shard_map/all_to_all | solution.py:510
  43.8 0.7 %correct.1 = (f32[16,512]{1,0:T(8,128)S(1)}, f32[16,2,128]{2,1,0:T(2,128)S(1)}) custom-call(f32[4,512]{1,0:T(4,128)S(1)} %get-tuple-element.12.mark_ref, s16[16,6,16,128]{3,2,1,0:T(8,128)(2,1)S(1)} %all_to_all.21.got_ref, s32[4,128]{1,0:T(4,128)S(1)} %get-tuple-element.18.degree_ref, bf16[1024,512]{1,0:T(8,128)(2,1)S(1)} %get-tuple-element.19.weight_ref), custom_call_target="tpu_custom_call" | custom-call | tf_op jit(solution)/shard_map/correct/pallas_call | solution.py:511
  44.6 11.2 %all_to_all.22.got_ref = f32[16,2,128]{2,1,0:T(2,128)S(1)} all-to-all(f32[16,2,128]{2,1,0:T(2,128)S(1)} %get-tuple-element.20), channel_id=1, replica_groups=mesh['z'=8,'core'=2,'col'=16] {'z','core'}, dimensions={0} | all-to-all | bytes 32768 | tf_op jit(solution)/shard_map/all_to_all | solution.py:518
  55.8 9.0 %all_to_all.23.got_ref = f32[16,2,128]{2,1,0:T(2,128)S(1)} all-to-all(f32[16,2,128]{2,1,0:T(2,128)S(1)} %add_up.1), channel_id=1, replica_groups=mesh['z'=8,'core'=2,'col'=16] {'col'}, dimensions={0} | all-to-all | bytes 32768 | tf_op jit(solution)/shard_map/all_to_all | solution.py:520
  64.8 1.0 %finish.1 = (f32[16,512]{1,0:T(8,128)}, f32[16,16]{1,0:T(8,128)}) custom-call(f32[16,2,128]{2,1,0:T(2,128)S(1)} %all_to_all.23.got_ref, f32[16,512]{1,0:T(8,128)S(1)} %get-tuple-element.21.image_ref), custom_call_target="tpu_custom_call" | custom-call | tf_op jit(solution)/shard_map/finish/pallas_call | solution.py:521
  (1 shorter events, 0.0 us)
Async XLA Ops:
  20.9 4.0 %collective-permute-start = (bf16[8,7,16,128]{3,2,1,0:T(8,128)(2,1)S(1)}, bf16[8,7,16,128]{3,2,1,0:T(8,128)(2,1)S(1)}, u32[]{:S(2)}, u32[]{:S(2)}) collective-permute-start(bf16[8,7,16,128]{3,2,1,0:T(8,128)(2,1)S(1)} %all_to_all.20.near_ref), channel_id=1, source_target_pairs={{0,16},{16,0},{1,17},{17,1},{2,18},{18,2},{3,19},{19,3},{4,20},{20... | collective-permute-start | bytes 688136 | tf_op jit(solution)/shard_map/ppermute | solution.py:483
